TPU v7x, 256 devices: a whole 4x4x8 slice. The times are simulated.
256 devices in a mesh: tm: 16 (over y_hi, x, core), rows: 16 (over z, y_lo).
Axes of the slice: x: 4, y: 4 (y_hi: 2, y_lo: 2; y = y_hi * 2 + y_lo), z: 8, core: 2. Of those that a mesh axis runs over, the one named last changes fastest.
Arguments:
- inputs: bfloat16 [16, 64, 120, 1024], P('tm', 'rows'), may hold values from -6 to 6
- hidden_one: bfloat16 [16, 64, 120, 256], P('tm', 'rows'), as said below
- hidden_two: bfloat16 [16, 64, 120, 256], P('tm', 'rows'), as said below
- outputs: bfloat16 [16, 64, 120, 1024], P('tm', 'rows'), as said below
- cotangent: bfloat16 [16, 64, 120, 1024], P('tm', 'rows'), may hold values from -6 to 6
- w_in: bfloat16 [1024, 256], replicated, may hold values from -0.1875 to 0.1875
- w_mid: bfloat16 [3, 3, 256, 256], replicated, may hold values from -0.125 to 0.125
- w_out: bfloat16 [256, 1024], replicated, may hold values from -0.375 to 0.375
Outputs:
- grad_inputs: bfloat16 [16, 64, 120, 1024], P('tm', 'rows')
- grad_w_in: float32 [1024, 256], P(('tm', 'rows'))
- grad_w_mid: float32 [3, 3, 65536], P(None, None, ('tm', 'rows'))
- grad_w_out: float32 [256, 1024], P(None, ('tm', 'rows'))
- grad_b_hidden: float32 [512], P(('tm', 'rows'))
- grad_b_out: float32 [1024], P(('tm', 'rows'))
Inputs may be any that keep to these rules, and one draw needn't show every extreme that they name: `hidden_one`: rectified values: zero in about half the entries, positive elsewhere. `hidden_two`: rectified values: zero in about half the entries, positive elsewhere. `outputs`: rectified values: zero in about half the entries, positive elsewhere.
All inputs are finite; a program needn't handle non-finite values.
Results may differ from a plain program's by a relative error of at most 0.013.
Values may be sent and summed in bfloat16 or wider, within the bound.
A program may use at most 384 MiB of HBM per device.

v0:
```python
import jax
import jax.numpy as jnp
from jax import lax
from jax.sharding import PartitionSpec as P


def padded(shard, sides, width):
    for axis, dim in sides:
        size, length = (lax.axis_size(axis), shard.shape[dim])
        up = [(i, (i + 1) % size) for i in range(size - 1)]
        down = [(j, i) for i, j in up]
        last = lax.slice_in_dim(shard, length - width, length, axis=dim)
        first = lax.slice_in_dim(shard, 0, width, axis=dim)
        before = lax.ppermute(last, axis, up)
        after = lax.ppermute(first, axis, down)
        shard = jnp.concatenate([before, shard, after], axis=dim)
    return shard


def on_device(inputs, hidden_one, hidden_two, outputs, cotangent, w_in, w_mid, w_out):
    frames = inputs.shape[0]
    band = inputs.shape[1]
    width = inputs.shape[2]
    chans = inputs.shape[3]
    mids = hidden_one.shape[3]
    shifted_width = chans // 8
    out_grad = jnp.where(outputs > 0, cotangent, jnp.zeros_like(cotangent))
    d_out = jnp.einsum("frwm,frwc->mc", hidden_two, out_grad, preferred_element_type=jnp.float32)
    b_out = jnp.sum(out_grad.astype(jnp.float32), (0, 1, 2))
    back_two = jnp.einsum("frwc,mc->frwm", out_grad, w_out, preferred_element_type=jnp.float32)
    mid_grad = jnp.where(hidden_two > 0, back_two, 0.0).astype(jnp.bfloat16)
    extended_one = padded(hidden_one, (("rows", 1),), 1)
    padded_one = jnp.pad(extended_one, ((0, 0), (0, 0), (1, 1), (0, 0)))
    kernel_rows = []
    for row_off in range(3):
        kernel_cols = []
        for col_off in range(3):
            window = padded_one[:, row_off : row_off + band, col_off : col_off + width]
            kernel_cols.append(
                jnp.einsum("frwi,frwo->io", window, mid_grad, preferred_element_type=jnp.float32)
            )
        kernel_rows.append(jnp.stack(kernel_cols, 0))
    d_mid = jnp.stack(kernel_rows, 0).reshape(3, 3, mids * mids)
    b_mid = jnp.sum(mid_grad.astype(jnp.float32), (0, 1, 2))
    extended_mid = padded(mid_grad, (("rows", 1),), 1)
    padded_mid = jnp.pad(extended_mid, ((0, 0), (0, 0), (1, 1), (0, 0)))
    back_one = jnp.zeros(hidden_one.shape, jnp.float32)
    for row_off in range(3):
        for col_off in range(3):
            source = padded_mid[
                :, 2 - row_off : 2 - row_off + band, 2 - col_off : 2 - col_off + width
            ]
            back_one = back_one + jnp.einsum(
                "frwo,io->frwi", source, w_mid[row_off, col_off], preferred_element_type=jnp.float32
            )
    first_grad = jnp.where(hidden_one > 0, back_one, 0.0).astype(jnp.bfloat16)
    extended_in = padded(inputs[:, :, :, : 2 * shifted_width], (("tm", 0),), 1)
    previous = extended_in[0:frames, :, :, :shifted_width]
    following = extended_in[2 : frames + 2, :, :, shifted_width:]
    shifted = jnp.concatenate([previous, following, inputs[:, :, :, 2 * shifted_width :]], -1)
    d_in = jnp.einsum("frwc,frwm->cm", shifted, first_grad, preferred_element_type=jnp.float32)
    b_in = jnp.sum(first_grad.astype(jnp.float32), (0, 1, 2))
    b_hidden = jnp.concatenate([b_in, b_mid], 0)
    extended_first = padded(first_grad, (("tm", 0),), 1)
    part_early = jnp.einsum(
        "frwm,cm->frwc",
        extended_first[2 : frames + 2],
        w_in[:shifted_width],
        preferred_element_type=jnp.float32,
    )
    part_late = jnp.einsum(
        "frwm,cm->frwc",
        extended_first[0:frames],
        w_in[shifted_width : 2 * shifted_width],
        preferred_element_type=jnp.float32,
    )
    part_rest = jnp.einsum(
        "frwm,cm->frwc", first_grad, w_in[2 * shifted_width :], preferred_element_type=jnp.float32
    )
    back_in = jnp.concatenate([part_early, part_late, part_rest], -1)
    grad_inputs = (out_grad.astype(jnp.float32) + back_in).astype(jnp.bfloat16)
    d_in, d_mid, d_out, b_hidden, b_out = (
        lax.psum_scatter(d_in, ("tm", "rows"), scatter_dimension=0, tiled=True),
        lax.psum_scatter(d_mid, ("tm", "rows"), scatter_dimension=2, tiled=True),
        lax.psum_scatter(d_out, ("tm", "rows"), scatter_dimension=1, tiled=True),
        lax.psum_scatter(b_hidden, ("tm", "rows"), scatter_dimension=0, tiled=True),
        lax.psum_scatter(b_out, ("tm", "rows"), scatter_dimension=0, tiled=True),
    )
    return (grad_inputs, d_in, d_mid, d_out, b_hidden, b_out)


def solution(mesh):
    placed = (
        P("tm", "rows", None, None),
        P("tm", "rows", None, None),
        P("tm", "rows", None, None),
        P("tm", "rows", None, None),
        P("tm", "rows", None, None),
        P(),
        P(),
        P(),
    )
    return jax.shard_map(
        on_device,
        mesh=mesh,
        in_specs=placed,
        out_specs=(
            P("tm", "rows", None, None),
            P(("tm", "rows"), None),
            P(None, None, ("tm", "rows")),
            P(None, ("tm", "rows")),
            P(("tm", "rows")),
            P(("tm", "rows")),
        ),
        check_vma=False,
    )
```

profile of v0, /device:TPU:0, one launch (start us, length us, event | category | flops | bytes accessed | tf_op | source)
XLA Modules:
  0.0 1681.0 jit_solution(8893674290369751251)
XLA Ops:
  7.2 1.7 slice.142
  8.9 1.3 collective-permute-start.5
  10.2 3.7 collective-permute-start.4
  14.0 0.9 fusion.75
  14.9 1.7 collective-permute-start.6
  16.6 1.3 collective-permute-start.7
  17.9 1.9 convert_reduce_fusion
  20.4 4.6 collective-permute-start
  24.9 1.5 convolution_bitcast_fusion.1
  26.8 1.0 stack.47
  27.8 1.3 collective-permute-start.1
  29.2 1.0 convolution_bitcast_fusion.10
  30.2 1.0 convolution_bitcast_fusion.9
  31.1 1.0 convolution_bitcast_fusion.7
  32.1 1.0 convolution_bitcast_fusion.6
  33.1 1.0 convolution_bitcast_fusion.4
  34.1 1.0 convolution_bitcast_fusion.12
  35.2 1.1 fusion.31
  36.3 1.2 fusion.24
  37.5 1.0 convolution_bitcast_fusion.5
  38.4 1.9 stack.51
  40.4 1.8 convolution_bitcast_fusion.11
  42.2 1.9 stack.43
  44.1 1.9 stack.44
  46.0 1.9 stack.46
  47.9 1.9 stack.48
  49.8 1.9 stack.50
  51.7 1.9 stack.42
  53.6 1.9 stack.52
  55.5 1.3 convolution_add_fusion.6
  56.8 1.2 convolution_add_fusion.5
  59.4 1.0 slice.165
  60.4 0.9 slice.164
  61.3 1.5 convolution_bitcast_fusion.2
  62.9 0.8 copy-done.3
  64.3 4.5 maximum_maximum_fusion
  68.8 80.5 %copy.16 = f32[3,3,65536]{1,0,2:T(4,128)} copy(f32[3,3,65536]{2,1,0:T(4,128)} %maximum_maximum_fusion) | data formatting | bytes 4718592
  149.3 124.9 %reshape.189 = f32[65536,9]{1,0:T(8,128)} reshape(f32[65536,3,3]{2,1,0:T(4,128)} %bitcast.64) | data formatting | bytes 4718592
  274.2 0.9 copy-done.11
  275.1 1.6 collective-permute-start.3
  276.7 1.3 collective-permute-start.2
  278.0 89.3 %all-reduce.6 = (f32[512]{0:T(512)S(1)}, f32[1024]{0:T(1024)S(1)}) all-reduce(f32[512]{0:T(512)S(1)} %pad_maximum_fusion.4, f32[1024]{0:T(1024)S(1)} %get-tuple-element.10), channel_id=5, replica_groups=mesh['tm'=16,'rows'=16] {'tm','rows'}, use_global_device_ids=true, to_apply=%region_5.6.clone | all-reduce | flops 1536 | bytes 12288
  369.4 1.2 fusion
  370.6 1.3 constant_dynamic-slice_fusion.1
  371.9 1.3 constant_dynamic-slice_fusion
  373.2 1299.0 %reduce-scatter.4.cloned.1.call-done = f32[256,9]{1,0:T(8,128)} async-done(((f32[65536,9]{1,0:T(8,128)}), f32[256,9]{1,0:T(8,128)}) %reduce-scatter.4.cloned.1.call-update) | async-done | bytes 9232
  1672.3 1.1 reshape.190
  1673.4 0.8 copy.17
  (64 shorter events, 5.1 us)
Async XLA Ops:
  7.2 12.7 copy-start
  7.2 12.7 copy-start.13
  7.2 363.4 %all-reduce.10.cloned.1.call-start = ((), (), s32[]{:S(2)}) async-start(), calls=%async_computation.2 | async-start | bytes 4194304
  8.9 50.4 %collective-permute-start.5 = (bf16[1,4,120,256]{3,2,1,0:T(8,128)(2,1)}, bf16[1,4,120,256]{3,2,1,0:T(8,128)(2,1)}, u32[]{:S(2)}, u32[]{:S(2)}) collective-permute-start(bf16[1,4,120,256]{3,2,1,0:T(8,128)(2,1)} %slice.142), channel_id=1, source_target_pairs={{16,0},{32,16},{48,32},{64,48},{80,64},{96,80},{112,96},{128,112},... | collective-permute-start | bytes 737288 | tf_op jit(solution)/shard_map/ppermute | solution.py:15
  10.2 50.1 %collective-permute-start.4 = (bf16[1,4,120,256]{3,2,1,0:T(8,128)(2,1)}, bf16[1,4,120,256]{3,2,1,0:T(8,128)(2,1)}, u32[]{:S(2)}, u32[]{:S(2)}) collective-permute-start(bf16[1,4,120,256]{3,2,1,0:T(8,128)(2,1)} %slice.142), channel_id=1, source_target_pairs={{0,16},{16,32},{32,48},{48,64},{64,80},{80,96},{96,112},{112,128},... | collective-permute-start | bytes 737288 | tf_op jit(solution)/shard_map/ppermute | solution.py:14
  14.9 12.9 collective-permute-start.6
  16.6 12.5 collective-permute-start.7
  19.9 6.6 copy-start.1
  20.4 14.7 collective-permute-start
  27.8 5.3 copy-start.14
  27.8 7.3 collective-permute-start.1
  29.1 4.0 copy-start.15
  34.1 3.4 copy-start.16
  55.5 2.4 copy-start.2
  58.8 2.6 slice-start
  59.4 2.0 copy-start.10
  62.8 0.9 copy-start.3
  62.8 1.0 copy-start.4
  62.8 1.1 copy-start.5
  62.8 1.2 copy-start.6
  62.8 1.3 copy-start.7
  62.8 1.3 copy-start.8
  62.9 1.4 copy-start.9
  62.9 1609.4 %reduce-scatter.4.cloned.1.call-start = ((), (), s32[]{:S(2)}) async-start(), calls=%async_computation.1 | async-start | bytes 33685504
  274.2 0.9 copy-start.11
  274.2 94.3 %copy-start.12 = (bf16[1024,256]{1,0:T(8,128)(2,1)S(1)}, bf16[1024,256]{1,0:T(8,128)(2,1)}, u32[]{:S(2)}) copy-start(bf16[1024,256]{1,0:T(8,128)(2,1)} %param.13) | copy-start | bytes 1572868
  275.1 93.8 %collective-permute-start.3 = (bf16[1,4,120,256]{3,2,1,0:T(8,128)(2,1)S(1)}, bf16[1,4,120,256]{3,2,1,0:T(8,128)(2,1)S(1)}, u32[]{:S(2)}, u32[]{:S(2)}) collective-permute-start(bf16[1,4,120,256]{3,2,1,0:T(8,128)(2,1)S(1)} %copy-done.11), channel_id=1, source_target_pairs={{0,16},{16,32},{32,48},{48,64},{64,80},{80,96},{96,112},{112,128},... | collective-permute-start | bytes 737288 | tf_op jit(solution)/shard_map/ppermute | solution.py:14
  276.7 92.4 %collective-permute-start.2 = (bf16[1,4,120,256]{3,2,1,0:T(8,128)(2,1)S(1)}, bf16[1,4,120,256]{3,2,1,0:T(8,128)(2,1)S(1)}, u32[]{:S(2)}, u32[]{:S(2)}) collective-permute-start(bf16[1,4,120,256]{3,2,1,0:T(8,128)(2,1)S(1)} %copy-done.11), channel_id=1, source_target_pairs={{16,0},{32,16},{48,32},{64,48},{80,64},{96,80},{112,96},{128,112},... | collective-permute-start | bytes 737288 | tf_op jit(solution)/shard_map/ppermute | solution.py:15
Sparse Core Ops, SparseCore 0:
  63.0 269.9 all-reduce.9
  335.5 1336.7 reduce-scatter.3
where the time goes:
time: 1690 us; the launch traced here: 1680 us
  waiting for transfers between devices  1300 us (77%)
  local copies, waits for them, and re-layouts  234 us (14%)
  blocking collectives  89.3 us (5%)
  matrix products  19.1 us (1%)
    unnamed x4, waiting for transfers between devices  1300 us
    unnamed x42, local copies, waits for them, and re-layouts  213 us
    unnamed x1, blocking collectives  89.3 us
  transfers between devices with their start and end apart: 10, of which 1 were waited for; matrix products, arithmetic and copies ran while one was open for 15% of the time, Pallas kernels for 0%

commit v1 on v0

v1 whole, which is shorter than its diff:
```python
import jax
import jax.numpy as jnp
from jax import lax
from jax.experimental import pallas as pl
from jax.experimental.pallas import tpu as pltpu
from jax.sharding import PartitionSpec as P

F32 = jnp.float32
BF16 = jnp.bfloat16
MESH = pl.DeviceIdType.MESH

BAND = 4
W = 120
WP = 128
NP = BAND * WP
C = 1024
M = 256
E = C // 8
PIECES = ((2, 2, 8), (5, 4, 24), (2, 3, 16))


def dot_t0(a, b):
    return lax.dot_general(a, b, (((0,), (0,)), ((), ())), preferred_element_type=F32)


def dot_t1(a, b):
    return lax.dot_general(a, b, (((1,), (1,)), ((), ())), preferred_element_type=F32)


def pad_rows(value):
    return jnp.concatenate([value, jnp.zeros((WP - W, value.shape[1]), F32)], 0).astype(BF16)


def kernel(
    inp, h1, h2, outp, cot, w_in, w_mid, w_out,
    gi_out, f0_out, f1_out, f2_out,
    inp_v, h1_v, h2_v, outp_v, cot_v, win_v, wmid_v, wout_v,
    og, h2p, h1x, m3, shifted, first, sprev, snext, h1up, h1dn, mup, mdn, mid_s,
    prod_e, prod_l, got_e, got_l, gi, back, d0, kf, d2, bo, bh,
    cs0, cr0, a1s0, a1r0, b1s0, b1r0, a2s0, a2r0, b2s0, b2r0, zs0, zr0,
    cs1, cr1, a1s1, a1r1, b1s1, b1r1, a2s1, a2r1, b2s1, b2r1, zs1, zr1,
    cs2, cr2, a1s2, a1r2, b1s2, b1r2, a2s2, a2r2, b2s2, b2r2, zs2, zr2,
    load_sem, send_sem, recv_sem,
):
    tm = lax.axis_index("tm")
    rows = lax.axis_index("rows")
    n_tm = lax.axis_size("tm")
    n_rows = lax.axis_size("rows")
    core = tm % 2
    mx = (tm // 2) % 4
    my = (tm // 8) * 2 + rows % 2
    mz = rows // 2

    def at(x, y, z, c):
        return (((y // 2) * 4 + x) * 2 + c, z * 2 + y % 2)

    sibling = at(mx, my, mz, 1 - core)
    x_peer = [at((mx + k) % 4, my, mz, core) for k in range(1, 4)]
    y_peer = [at(mx, (my + k) % 4, mz, core) for k in range(1, 4)]
    z_peer = [at(mx, my, (mz + k) % 8, core) for k in range(1, 8)]
    tm_next = ((tm + 1) % n_tm, rows)
    tm_prev = ((tm + n_tm - 1) % n_tm, rows)
    row_next = (tm, (rows + 1) % n_rows)
    row_prev = (tm, (rows + n_rows - 1) % n_rows)

    loads = []
    for i, (src, dst) in enumerate(
        ((outp, outp_v), (cot, cot_v), (w_out, wout_v), (h2, h2_v), (h1, h1_v), (w_mid, wmid_v), (inp, inp_v), (w_in, win_v))
    ):
        copy = pltpu.make_async_copy(src, dst, load_sem.at[i])
        copy.start()
        loads.append(copy)

    barrier = pltpu.get_barrier_semaphore()
    partners = [sibling, *x_peer, *y_peer, *z_peer, tm_next, tm_prev, row_next, row_prev]
    for peer in partners:
        pl.semaphore_signal(barrier, inc=1, device_id=peer, device_id_type=MESH)

    counter = [0]

    def send(src, dst, peer):
        i = counter[0]
        counter[0] += 1
        copy = pltpu.make_async_remote_copy(
            src_ref=src, dst_ref=dst, send_sem=send_sem.at[i], recv_sem=recv_sem.at[i],
            device_id=peer, device_id_type=MESH,
        )
        copy.start()
        return copy

    for copy in loads[:4]:
        copy.wait()
    for r in range(BAND):
        grad = jnp.where(outp_v[r].astype(F32) > 0, cot_v[r].astype(F32), 0.0)
        og[r * WP : (r + 1) * WP, :] = pad_rows(grad)
        h2p[r * WP : (r + 1) * WP, :] = pad_rows(h2_v[r].astype(F32))
    mid32 = jnp.where(h2p[...].astype(F32) > 0, dot_t1(og[...], wout_v[...]), 0.0)
    mid_s[...] = mid32.astype(BF16)
    m3[WP : WP + NP, 0:M] = pltpu.roll(mid32, NP - 1, 0).astype(BF16)
    m3[WP : WP + NP, M : 2 * M] = mid_s[...]
    m3[WP : WP + NP, 2 * M : 3 * M] = pltpu.roll(mid32, 1, 0).astype(BF16)
    ones = jnp.ones((NP, WP), BF16)
    grad = dot_t0(og[...], h2p[...])
    for h in range(2):
        d0[h] = grad[:, h * 128 : (h + 1) * 128].reshape(16, 64, 128)
    bo[...] = dot_t0(og[...], ones).reshape(16, 64, WP)
    bh[8:16] = dot_t0(mid_s[...], ones).reshape(8, 32, WP)

    pl.semaphore_wait(barrier, len(partners))
    mid_down = send(mid_s.at[pl.ds((BAND - 1) * WP, WP)], mup, row_next)
    mid_up = send(mid_s.at[pl.ds(0, WP)], mdn, row_prev)
    one_down = send(h1.at[BAND - 1], h1up, row_next)
    one_up = send(h1.at[0], h1dn, row_prev)
    in_next = send(inp.at[:, :, pl.ds(0, E)], sprev, tm_next)
    in_prev = send(inp.at[:, :, pl.ds(E, E)], snext, tm_prev)

    def slab(piece, t, low, s):
        if piece == 1:
            parts = [kf[2 * s + h, t, pl.ds(low, 8, stride=2), :] for h in range(2)]
        elif s < 4:
            held = d0 if piece == 0 else d2
            parts = [held[h, t, pl.ds(4 * low + s, 8, stride=8), :] for h in range(2)]
        else:
            lane = lax.broadcasted_iota(jnp.int32, (8, 128), 1)
            total = jnp.zeros((8, 128), F32)
            for j in range(4):
                total = jnp.where(lane == j, bo[t, pl.ds(4 * low + j, 8, stride=8), :], total)
            for j in range(2):
                total = jnp.where(lane == 4 + j, bh[t, pl.ds(2 * low + j, 8, stride=4), :], total)
            parts = [total, jnp.zeros((8, 128), F32)]
        return jnp.concatenate(parts, 0)

    def two_terms(value):
        total = value[0:8] + value[8:16]
        head = total.astype(BF16).astype(F32)
        return jnp.concatenate([head, total - head], 0)

    bufs = (
        (cs0, cr0, a1s0, a1r0, b1s0, b1r0, a2s0, a2r0, b2s0, b2r0, zs0, zr0),
        (cs1, cr1, a1s1, a1r1, b1s1, b1r1, a2s1, a2r1, b2s1, b2r1, zs1, zr1),
        (cs2, cr2, a1s2, a1r2, b1s2, b1r2, a2s2, a2r2, b2s2, b2r2, zs2, zr2),
    )

    def core_phase(p):
        na, nb, _ = PIECES[p]
        cs, cr = bufs[p][:2]

        def body(x, carry):
            for y in range(4):
                t = ((y // 2) * 4 + x) * 2 + (1 - core)
                for s in range(na + nb):
                    value = slab(p, t, y % 2, s)
                    if p == 2 and s == 4:
                        value = two_terms(value)
                    cs[x, y, s] = value.astype(BF16)
            return carry

        lax.fori_loop(0, 4, body, 0)
        return [send(cs, cr, sibling)]

    def first_phase(p, copies):
        na, nb, _ = PIECES[p]
        cs, cr, a1s, a1r, b1s, b1r = bufs[p][:6]
        for copy in copies:
            copy.wait()

        def body(x, carry):
            for y in range(4):
                t = ((y // 2) * 4 + x) * 2 + core
                for s in range(na + nb):
                    value = slab(p, t, y % 2, s) + cr[x, y, s].astype(F32)
                    if p == 2 and s == 4:
                        value = two_terms(value)
                    if s < na:
                        a1s[x, y, s] = value.astype(BF16)
                    else:
                        b1s[y, x, s - na] = value.astype(BF16)
            return carry

        lax.fori_loop(0, 4, body, 0)
        out = []
        for k in (2, 1, 3):
            out.append(send(a1s.at[(mx + k) % 4], a1r.at[k - 1], x_peer[k - 1]))
            out.append(send(b1s.at[(my + k) % 4], b1r.at[k - 1], y_peer[k - 1]))
        return out

    def gathered(own, held, got, j):
        total = held[own, j].astype(F32)
        for k in range(3):
            total = total + got[k, j].astype(F32)
        return total

    def second_phase(p, copies):
        na, nb, _ = PIECES[p]
        _, _, a1s, a1r, b1s, b1r, a2s, a2r, b2s, b2r = bufs[p][:10]
        for copy in copies:
            copy.wait()
        for j in range(4):
            a2s[j] = gathered(mx, a1s, a1r, j).astype(BF16)
            total = gathered(my, b1s, b1r, j)
            for s in range(nb):
                value = total[s]
                if p == 2 and s == nb - 1:
                    value = two_terms(value)
                b2s[j, s] = value.astype(BF16)
        out = []
        for k in (2, 1, 3):
            out.append(send(a2s.at[(my + k) % 4], a2r.at[k - 1], y_peer[k - 1]))
            out.append(send(b2s.at[(mx + k) % 4], b2r.at[k - 1], x_peer[k - 1]))
        return out

    def third_phase(p, copies):
        na, nb, depth = PIECES[p]
        _, _, _, _, _, _, a2s, a2r, b2s, b2r, zs, zr = bufs[p]
        for copy in copies:
            copy.wait()
        for s in range(na + nb):
            own, held, got, j = (my, a2s, a2r, s) if s < na else (mx, b2s, b2r, s - na)
            total = gathered(own, held, got, j)
            for h in range(2):
                zs[pl.ds(2 * s + h, 8, stride=depth), :] = total[8 * h : 8 * h + 8]
        out = []
        for k in (4, 3, 5, 2, 6, 1, 7):
            start = pl.multiple_of(((mz + k) % 8) * depth, 8)
            out.append(send(zs.at[pl.ds(start, depth)], zr.at[k - 1], z_peer[k - 1]))
        return out

    def last_phase(p, copies, result):
        depth = PIECES[p][2]
        zs, zr = bufs[p][10:]
        for copy in copies:
            copy.wait()
        total = zs[pl.ds(pl.multiple_of(mz * depth, 8), depth), :]
        for k in range(7):
            total = total + zr[k]
        result[...] = total

    flight0 = core_phase(0)

    loads[5].wait()
    w = [[wmid_v[a, b] for b in range(3)] for a in range(3)]

    def back_of(start, count, a):
        total = None
        for b in range(3):
            term = dot_t1(m3[start : start + count, b * M : (b + 1) * M], w[a][b])
            total = term if total is None else total + term
        return total

    back[...] = back_of(WP, NP, 1)
    back[0 : NP - WP, :] += back_of(2 * WP, NP - WP, 0)
    back[WP:NP, :] += back_of(WP, NP - WP, 2)

    flight0 = first_phase(0, flight0)

    loads[4].wait()
    one_down.wait()
    one_up.wait()
    for r in range(BAND):
        h1x[(r + 1) * WP : (r + 2) * WP, :] = pad_rows(h1_v[r].astype(F32))
    h1x[0:WP, :] = pad_rows(jnp.where(rows > 0, h1up[...].astype(F32), 0.0))
    h1x[NP + WP : NP + 2 * WP, :] = pad_rows(jnp.where(rows < n_rows - 1, h1dn[...].astype(F32), 0.0))
    for a in range(3):
        grad = dot_t0(h1x[a * WP : a * WP + NP, :], m3[WP : WP + NP, :])
        for h in range(6):
            kf[6 * a + h] = grad[:, h * 128 : (h + 1) * 128].reshape(16, 16, 128)
    flight1 = core_phase(1)

    mid_down.wait()
    mid_up.wait()
    up = jnp.where(rows > 0, mup[...].astype(F32), 0.0)
    down = jnp.where(rows < n_rows - 1, mdn[...].astype(F32), 0.0)
    for value, start in ((up, 0), (down, NP + WP)):
        m3[start : start + WP, 0:M] = pltpu.roll(value, WP - 1, 0).astype(BF16)
        m3[start : start + WP, M : 2 * M] = value.astype(BF16)
        m3[start : start + WP, 2 * M : 3 * M] = pltpu.roll(value, 1, 0).astype(BF16)
    back[0:WP, :] += back_of(0, WP, 2)
    back[NP - WP : NP, :] += back_of(NP + WP, WP, 0)
    first[...] = jnp.where(h1x[WP : WP + NP, :].astype(F32) > 0, back[...], 0.0).astype(BF16)

    loads[6].wait()
    loads[7].wait()
    in_next.wait()
    in_prev.wait()
    for r in range(BAND):
        part = slice(r * WP, (r + 1) * WP)
        shifted[part, 0:E] = pad_rows(jnp.where(tm > 0, sprev[r].astype(F32), 0.0))
        shifted[part, E : 2 * E] = pad_rows(jnp.where(tm < n_tm - 1, snext[r].astype(F32), 0.0))
        shifted[part, 2 * E :] = pad_rows(inp_v[r, :, 2 * E :].astype(F32))
    grad = dot_t0(shifted[...], first[...])
    for h in range(2):
        d2[h] = grad[:, h * 128 : (h + 1) * 128].reshape(16, 64, 128)
    bh[0:8] = dot_t0(first[...], ones).reshape(8, 32, WP)
    flight2 = core_phase(2)

    prod_e[...] = dot_t1(first[...], win_v[0:E, :]).astype(BF16)
    early = send(prod_e, got_e, tm_prev)
    prod_l[...] = dot_t1(first[...], win_v[E : 2 * E, :]).astype(BF16)
    late = send(prod_l, got_l, tm_next)

    flight1 = first_phase(1, flight1)
    flight2 = first_phase(2, flight2)
    flight0 = second_phase(0, flight0)

    rest = og[:, 2 * E :].astype(F32) + dot_t1(first[...], win_v[2 * E :, :])
    for r in range(BAND):
        gi[r, :, 2 * E :] = rest[r * WP : r * WP + W].astype(BF16)
    early.wait()
    late.wait()
    for r in range(BAND):
        part = slice(r * WP, r * WP + WP)
        one = og[part, 0:E].astype(F32) + jnp.where(tm < n_tm - 1, got_e[part, :].astype(F32), 0.0)
        two = og[part, E : 2 * E].astype(F32) + jnp.where(tm > 0, got_l[part, :].astype(F32), 0.0)
        gi[r, :, 0:E] = one[:W].astype(BF16)
        gi[r, :, E : 2 * E] = two[:W].astype(BF16)
    store = pltpu.make_async_copy(gi, gi_out, load_sem.at[8])
    store.start()

    flight0 = third_phase(0, flight0)
    flight1 = second_phase(1, flight1)
    flight2 = second_phase(2, flight2)
    flight1 = third_phase(1, flight1)
    flight2 = third_phase(2, flight2)
    last_phase(0, flight0, f0_out)
    last_phase(1, flight1, f1_out)
    last_phase(2, flight2, f2_out)
    store.wait()


def scratch():
    def v(*shape, dtype=BF16):
        return pltpu.VMEM(shape, dtype)

    shapes = [
        v(BAND, W, C), v(BAND, W, M), v(BAND, W, M), v(BAND, W, C), v(BAND, W, C),
        v(C, M), v(3, 3, M, M), v(M, C),
        v(NP, C), v(NP, M), v(NP + 2 * WP, M), v(NP + 2 * WP, 3 * M), v(NP, C), v(NP, M),
        v(BAND, W, E), v(BAND, W, E), v(W, M), v(W, M), v(WP, M), v(WP, M), v(NP, M),
        v(NP, E), v(NP, E), v(NP, E), v(NP, E), v(BAND, W, C),
        v(NP, M, dtype=F32), v(2, 16, 64, 128, dtype=F32), v(18, 16, 16, 128, dtype=F32), v(2, 16, 64, 128, dtype=F32),
        v(16, 64, WP, dtype=F32), v(16, 32, WP, dtype=F32),
    ]
    for na, nb, depth in PIECES:
        tile = (16, 128)
        shapes += [v(4, 4, na + nb, *tile), v(4, 4, na + nb, *tile)]
        shapes += [v(4, 4, na, *tile), v(3, 4, na, *tile), v(4, 4, nb, *tile), v(3, 4, nb, *tile)]
        shapes += [v(4, na, *tile), v(3, na, *tile), v(4, nb, *tile), v(3, nb, *tile)]
        shapes += [v(8 * depth, 128, dtype=F32), v(7, depth, 128, dtype=F32)]
    shapes += [pltpu.SemaphoreType.DMA((9,)), pltpu.SemaphoreType.DMA((80,)), pltpu.SemaphoreType.DMA((80,))]
    return shapes


def finish(f0, f1, f2, d_in, d_mid, d_out, b_hidden, b_out):
    def lines(ref, start, count):
        return jnp.concatenate([ref[pl.ds(2 * start + h, count, stride=2), :] for h in range(2)], 1)

    d_in[...] = lines(f2, 0, 4)
    for a in range(3):
        d_mid[a] = lines(f1, 3 * a, 3)
    d_out[...] = lines(f0, 0, 4)
    bias = f2[8:9, :] + f2[9:10, :]
    b_hidden[...] = bias
    b_out[...] = bias


def on_device(inputs, hidden_one, hidden_two, outputs, cotangent, w_in, w_mid, w_out):
    anywhere = pl.BlockSpec(memory_space=pl.ANY)
    vmem = pl.BlockSpec(memory_space=pltpu.VMEM)
    gi, f0, f1, f2 = pl.pallas_call(
        kernel,
        out_shape=[
            jax.ShapeDtypeStruct((BAND, W, C), BF16),
            jax.ShapeDtypeStruct((PIECES[0][2], 128), F32),
            jax.ShapeDtypeStruct((PIECES[1][2], 128), F32),
            jax.ShapeDtypeStruct((PIECES[2][2], 128), F32),
        ],
        in_specs=[anywhere] * 8,
        out_specs=[anywhere, vmem, vmem, vmem],
        scratch_shapes=scratch(),
        compiler_params=pltpu.CompilerParams(
            collective_id=0, has_side_effects=True, vmem_limit_bytes=56 * 2**20
        ),
    )(inputs[0], hidden_one[0], hidden_two[0], outputs[0], cotangent[0], w_in, w_mid, w_out)
    d_in, d_mid, d_out, b_hidden, b_out = pl.pallas_call(
        finish,
        out_shape=[
            jax.ShapeDtypeStruct((4, M), F32),
            jax.ShapeDtypeStruct((3, 3, M), F32),
            jax.ShapeDtypeStruct((4, M), F32),
            jax.ShapeDtypeStruct((1, 128), F32),
            jax.ShapeDtypeStruct((1, 128), F32),
        ],
        in_specs=[vmem] * 3,
        out_specs=[vmem] * 5,
    )(f0, f1, f2)
    return gi[None], d_in, d_mid, d_out.T, b_hidden[0, 4:6], b_out[0, 0:4]


def solution(mesh):
    placed = (
        P("tm", "rows", None, None),
        P("tm", "rows", None, None),
        P("tm", "rows", None, None),
        P("tm", "rows", None, None),
        P("tm", "rows", None, None),
        P(),
        P(),
        P(),
    )
    return jax.shard_map(
        on_device,
        mesh=mesh,
        in_specs=placed,
        out_specs=(
            P("tm", "rows", None, None),
            P(("tm", "rows"), None),
            P(None, None, ("tm", "rows")),
            P(None, ("tm", "rows")),
            P(("tm", "rows")),
            P(("tm", "rows")),
        ),
        check_vma=False,
    )
```

time: 1690 us -> 49.4 us (0.03)
  the two profiles are of different devices: /device:TPU:0 before, /device:TPU:2 now
where the time goes in v1:
time: 49.4 us; the launch traced here: 49.2 us
  Pallas kernels  43.9 us (89%)
  local copies, waits for them, and re-layouts  4.61 us (9%)
  between operations  0.64 us (1%)
    pallas_call x1, Pallas kernels, on_device(): pl.pallas_call(kernel, out_shape=[jax.ShapeDtypeStruct((BAND, W, C), BF16...  42.6 us
    squeeze x2, local copies, waits for them, and re-layouts, on_device(): return (gi[None], d_in, d_mid, d_out.T, b_hidden[0, 4:6], b_out[0, 0:4])  2.4 us
    unnamed x1, local copies, waits for them, and re-layouts  2.21 us
    pallas_call x1, Pallas kernels, on_device(): pl.pallas_call(finish, out_shape=[jax.ShapeDtypeStruct((4, M), F32), jax....  1.33 us

profile of v1, /device:TPU:2, one launch (start us, length us, event | category | flops | bytes accessed | tf_op | source)
XLA Modules:
  0.0 49.2 jit_solution(6793714942523594874)
XLA Ops:
  0.6 42.6 %shard_map.127 = (bf16[4,120,1024]{2,1,0:T(8,128)(2,1)}, f32[8,128]{1,0:T(8,128)}, f32[24,128]{1,0:T(8,128)}, f32[16,128]{1,0:T(8,128)}) custom-call(bf16[4,120,1024]{2,1,0:T(8,128)(2,1)} %bitcast.11, bf16[4,120,256]{2,1,0:T(8,128)(2,1)} %bitcast.15, bf16[4,120,256]{2,1,0:T(8,128)(2,1)} %bitcast.16, bf16[4,120,1024]{2,1,0:T(8,128)(2,1)} %bitcast.12, ...), custom_call_target="tpu_custom_call" | custom-call | tf_op jit(solution)/shard_map/pallas_call | solution.py:369
  43.2 1.3 %shard_map.128 = (f32[4,256]{1,0:T(4,128)}, f32[3,3,256]{2,1,0:T(4,128)}, f32[4,256]{1,0:T(4,128)}, f32[1,128]{1,0:T(1,128)}, f32[1,128]{1,0:T(1,128)}) custom-call(f32[8,128]{1,0:T(8,128)} %get-tuple-element.16.f0, f32[24,128]{1,0:T(8,128)} %get-tuple-element.17.f1, f32[16,128]{1,0:T(8,128)} %get-tuple-element.18.f2), custom_call_target="tpu_custom_call" | custom-call | tf_op jit(solution)/shard_map/pallas_call | solution.py:384
  44.6 1.2 %slice_bitcast_fusion = f32[4]{0:T(128)} fusion(f32[1,128]{1,0:T(1,128)} %get-tuple-element.23), kind=kLoop, calls=%fused_computation | loop fusion | bytes 32 | tf_op jit(solution)/shard_map/squeeze | solution.py:396
  45.7 1.2 %slice_bitcast_fusion.1 = f32[2]{0:T(128)} fusion(f32[1,128]{1,0:T(1,128)} %get-tuple-element.22), kind=kLoop, calls=%fused_computation.1 | loop fusion | bytes 16 | tf_op jit(solution)/shard_map/squeeze | solution.py:396
  47.0 2.2 %copy.15 = bf16[1,4,120,1024]{3,2,1,0:T(8,128)(2,1)} copy(bf16[1,4,120,1024]{3,2,1,0:T(8,128)(2,1)} %bitcast.14) | data formatting | bytes 1966080

commit v2 on v1

v2 whole, which is shorter than its diff:
```python
import jax
import jax.numpy as jnp
from jax import lax
from jax.experimental import pallas as pl
from jax.experimental.pallas import tpu as pltpu
from jax.sharding import PartitionSpec as P

F32 = jnp.float32
BF16 = jnp.bfloat16
MESH = pl.DeviceIdType.MESH

BAND = 4
W = 120
WP = 128
NP = BAND * WP
C = 1024
M = 256
E = C // 8
PIECES = ((4, 3, 16), (3, 3, 16), (5, 0, 16))


def dot_t0(a, b):
    return lax.dot_general(a, b, (((0,), (0,)), ((), ())), preferred_element_type=F32)


def dot_t1(a, b):
    return lax.dot_general(a, b, (((1,), (1,)), ((), ())), preferred_element_type=F32)


def pad_rows(value):
    return jnp.concatenate([value, jnp.zeros((WP - W, value.shape[1]), F32)], 0).astype(BF16)


def kernel(
    inp, h1, h2, outp, cot, w_in, w_mid, w_out,
    gi_out, f0_out, f1_out, f2_out,
    inp_v, h1_v, h2_v, outp_v, cot_v, win_v, wmid_v, wout_v,
    og, og_t, h2o, h1p, h1_t, m3, in_t, edge_t, first, mid_s, edge_mid, mup, mdn,
    prod_e, prod_l, got_e, got_l, gi, back, d0, kf, d2, bo, bh,
    cs0, cr0, a1s0, a1r0, b1s0, b1r0, a2s0, a2r0, b2s0, b2r0, zs0, zr0,
    cs1, cr1, a1s1, a1r1, b1s1, b1r1, a2s1, a2r1, b2s1, b2r1, zs1, zr1,
    cs2, cr2, xys2, xyr2, zs2, zr2,
    load_sem, send_sem, recv_sem,
):
    tm = lax.axis_index("tm")
    rows = lax.axis_index("rows")
    n_tm = lax.axis_size("tm")
    n_rows = lax.axis_size("rows")
    core = tm % 2
    mx = (tm // 2) % 4
    my = (tm // 8) * 2 + rows % 2
    mz = rows // 2

    def at(x, y, z, c):
        return (((y // 2) * 4 + x) * 2 + c, z * 2 + y % 2)

    sibling = at(mx, my, mz, 1 - core)
    xy_peer = {(i, j): at((mx + i) % 4, (my + j) % 4, mz, core) for i in range(4) for j in range(4) if i + j}
    x_peer = [xy_peer[k, 0] for k in range(1, 4)]
    y_peer = [xy_peer[0, k] for k in range(1, 4)]
    z_peer = [at(mx, my, (mz + k) % 8, core) for k in range(1, 8)]
    tm_next = ((tm + 1) % n_tm, rows)
    tm_prev = ((tm + n_tm - 1) % n_tm, rows)
    row_next = (tm, (rows + 1) % n_rows)
    row_prev = (tm, (rows + n_rows - 1) % n_rows)

    loads = []
    for i, (src, dst) in enumerate(
        ((outp, outp_v), (cot, cot_v), (w_out, wout_v), (h2, h2_v), (h1, h1_v), (inp, inp_v), (w_mid, wmid_v), (w_in, win_v))
    ):
        copy = pltpu.make_async_copy(src, dst, load_sem.at[i])
        copy.start()
        loads.append(copy)

    barrier = pltpu.get_barrier_semaphore()
    partners = [sibling, *xy_peer.values(), *z_peer, tm_next, tm_prev, row_next, row_prev]
    for peer in partners:
        pl.semaphore_signal(barrier, inc=1, device_id=peer, device_id_type=MESH)

    counter = [0]

    def send(src, dst, peer):
        i = counter[0]
        counter[0] += 1
        copy = pltpu.make_async_remote_copy(
            src_ref=src, dst_ref=dst, send_sem=send_sem.at[i], recv_sem=recv_sem.at[i],
            device_id=peer, device_id_type=MESH,
        )
        copy.start()
        return copy

    def dot(a, b):
        return jnp.dot(a, b, preferred_element_type=F32)

    def halves(held, value, *shape):
        for h in range(value.shape[1] // 128):
            held[h] = value[:, h * 128 : (h + 1) * 128].reshape(*shape, 128)

    def as_column(value):
        total = jnp.sum(value.astype(F32), 0, keepdims=True)
        return jnp.broadcast_to(total, (WP, M)).T.reshape(8, 32, WP)

    for copy in loads[:4]:
        copy.wait()
    for r in range(BAND):
        grad = jnp.where(outp_v[r].astype(F32) > 0, cot_v[r].astype(F32), 0.0)
        og[r * WP : (r + 1) * WP, :] = pad_rows(grad)
        h2o[r * WP : (r + 1) * WP, 0:M] = pad_rows(h2_v[r].astype(F32))
    h2o[:, M:] = jnp.ones((NP, WP), BF16)
    mid32 = jnp.where(h2o[:, 0:M].astype(F32) > 0, dot_t1(og[...], wout_v[...]), 0.0)
    mid = mid32.astype(BF16)
    mid_s[...] = mid
    edge_mid[0] = jnp.where(rows < n_rows - 1, mid32[NP - WP :], 0.0).astype(BF16)
    edge_mid[1] = jnp.where(rows > 0, mid32[:WP], 0.0).astype(BF16)
    m3[WP : WP + NP, 0:M] = pltpu.roll(mid32, NP - 1, 0).astype(BF16)
    m3[WP : WP + NP, M : 2 * M] = mid
    m3[WP : WP + NP, 2 * M : 3 * M] = pltpu.roll(mid32, 1, 0).astype(BF16)

    og_t[...] = og[...].T
    grad = dot(og_t[...], h2o[...])
    halves(d0, grad[:, 0:M], 16, 64)
    bo[...] = grad[:, M:].reshape(16, 64, WP)
    bh[8:16] = as_column(mid)
    loads[4].wait()
    for r in range(BAND):
        h1p[r * WP : (r + 1) * WP, :] = pad_rows(h1_v[r].astype(F32))
    h1_t[...] = h1p[...].T
    halves(kf.at[pl.ds(6, 6)], dot(h1_t[...], m3[WP : WP + NP, :]), 16, 16)
    loads[5].wait()
    for r in range(BAND):
        part = slice(r * WP, (r + 1) * WP)
        value = pad_rows(inp_v[r].astype(F32)).T
        edge_t[0, :, part] = jnp.where(tm < n_tm - 1, value[0:E].astype(F32), 0.0).astype(BF16)
        edge_t[1, :, part] = jnp.where(tm > 0, value[E : 2 * E].astype(F32), 0.0).astype(BF16)
        in_t[2 * E :, part] = value[2 * E :]

    pl.semaphore_wait(barrier, len(partners))
    mid_down = send(edge_mid.at[0], mup, row_next)
    mid_up = send(edge_mid.at[1], mdn, row_prev)
    in_next = send(edge_t.at[0], in_t.at[pl.ds(0, E)], tm_next)
    in_prev = send(edge_t.at[1], in_t.at[pl.ds(E, E)], tm_prev)

    def slab(piece, t, low, s):
        if piece == 0 and s >= 4 or piece == 1:
            tap = s - 1 if piece == 0 else s if s < 3 else s + 3
            parts = [kf[2 * tap + h, t, pl.ds(low, 8, stride=2), :] for h in range(2)]
        elif s < 4:
            held = d0 if piece == 0 else d2
            parts = [held[h, t, pl.ds(4 * low + s, 8, stride=8), :] for h in range(2)]
        else:
            lane = lax.broadcasted_iota(jnp.int32, (8, 128), 1)
            total = jnp.zeros((8, 128), F32)
            for j in range(4):
                total = jnp.where(lane == j, bo[t, pl.ds(4 * low + j, 8, stride=8), :], total)
            for j in range(2):
                total = jnp.where(lane == 4 + j, bh[t, pl.ds(2 * low + j, 8, stride=4), :], total)
            parts = [total, jnp.zeros((8, 128), F32)]
        return jnp.concatenate(parts, 0)

    def two_terms(value):
        total = value[0:8] + value[8:16]
        head = total.astype(BF16).astype(F32)
        return jnp.concatenate([head, total - head], 0)

    bufs = (
        (cs0, cr0, a1s0, a1r0, b1s0, b1r0, a2s0, a2r0, b2s0, b2r0, zs0, zr0),
        (cs1, cr1, a1s1, a1r1, b1s1, b1r1, a2s1, a2r1, b2s1, b2r1, zs1, zr1),
        (cs2, cr2, xys2, xyr2, None, None, None, None, None, None, zs2, zr2),
    )

    def core_phase(p):
        na, nb, _ = PIECES[p]
        cs, cr = bufs[p][:2]

        def body(x, carry):
            for y in range(4):
                t = ((y // 2) * 4 + x) * 2 + (1 - core)
                for s in range(na + nb):
                    value = slab(p, t, y % 2, s)
                    if p == 2 and s == 4:
                        value = two_terms(value)
                    cs[x, y, s] = value.astype(BF16)
            return carry

        lax.fori_loop(0, 4, body, 0)
        return [send(cs, cr, sibling)]

    def first_phase(p, copies):
        na, nb, _ = PIECES[p]
        cs, cr, a1s, a1r, b1s, b1r = bufs[p][:6]
        for copy in copies:
            copy.wait()

        def body(x, carry):
            for y in range(4):
                t = ((y // 2) * 4 + x) * 2 + core
                for s in range(na + nb):
                    value = slab(p, t, y % 2, s) + cr[x, y, s].astype(F32)
                    if p == 2 and s == 4:
                        value = two_terms(value)
                    if s < na:
                        a1s[x, y, s] = value.astype(BF16)
                    else:
                        b1s[y, x, s - na] = value.astype(BF16)
            return carry

        lax.fori_loop(0, 4, body, 0)
        out = []
        if p == 2:
            for (i, j), peer in sorted(xy_peer.items(), key=lambda item: -(item[0][0] % 3 + item[0][1] % 3)):
                out.append(send(a1s.at[(mx + i) % 4, (my + j) % 4], a1r.at[4 * i + j - 1], peer))
            return out
        for k in (2, 1, 3):
            out.append(send(a1s.at[(mx + k) % 4], a1r.at[k - 1], x_peer[k - 1]))
            out.append(send(b1s.at[(my + k) % 4], b1r.at[k - 1], y_peer[k - 1]))
        return out

    def gathered(own, held, got, j):
        total = held[own, j].astype(F32)
        for k in range(3):
            total = total + got[k, j].astype(F32)
        return total

    def second_phase(p, copies):
        na, nb, _ = PIECES[p]
        _, _, a1s, a1r, b1s, b1r, a2s, a2r, b2s, b2r = bufs[p][:10]
        for copy in copies:
            copy.wait()
        for j in range(4):
            a2s[j] = gathered(mx, a1s, a1r, j).astype(BF16)
            b2s[j] = gathered(my, b1s, b1r, j).astype(BF16)
        out = []
        for k in (2, 1, 3):
            out.append(send(a2s.at[(my + k) % 4], a2r.at[k - 1], y_peer[k - 1]))
            out.append(send(b2s.at[(mx + k) % 4], b2r.at[k - 1], x_peer[k - 1]))
        return out

    def third_phase(p, copies):
        na, nb, depth = PIECES[p]
        _, _, xys, xyr, _, _, a2s, a2r, b2s, b2r, zs, zr = bufs[p]
        for copy in copies:
            copy.wait()
        for s in range(na + nb):
            if p == 2:
                total = xys[mx, my, s].astype(F32)
                for k in range(15):
                    total = total + xyr[k, s].astype(F32)
            else:
                own, held, got, j = (my, a2s, a2r, s) if s < na else (mx, b2s, b2r, s - na)
                total = gathered(own, held, got, j)
            for h in range(2):
                zs[pl.ds(2 * s + h, 8, stride=depth), :] = total[8 * h : 8 * h + 8]
        out = []
        for k in (4, 3, 5, 2, 6, 1, 7):
            start = pl.multiple_of(((mz + k) % 8) * depth, 8)
            out.append(send(zs.at[pl.ds(start, depth)], zr.at[k - 1], z_peer[k - 1]))
        return out

    def last_phase(p, copies, result):
        depth = PIECES[p][2]
        zs, zr = bufs[p][10:]
        for copy in copies:
            copy.wait()
        total = zs[pl.ds(pl.multiple_of(mz * depth, 8), depth), :]
        for k in range(7):
            total = total + zr[k]
        result[...] = total

    flight0 = core_phase(0)

    def back_of(start, count, a):
        total = None
        for b in range(3):
            term = dot_t1(m3[start : start + count, b * M : (b + 1) * M], wmid_v[a, b])
            total = term if total is None else total + term
        return total

    loads[6].wait()
    back[...] = back_of(WP, NP, 1)
    back[0 : NP - WP, :] += back_of(2 * WP, NP - WP, 0)
    back[WP:NP, :] += back_of(WP, NP - WP, 2)

    flight0 = first_phase(0, flight0)

    mid_down.wait()
    mid_up.wait()
    for held, start in ((mup, 0), (mdn, NP + WP)):
        value = held[...].astype(F32)
        m3[start : start + WP, 0:M] = pltpu.roll(value, WP - 1, 0).astype(BF16)
        m3[start : start + WP, M : 2 * M] = held[...]
        m3[start : start + WP, 2 * M : 3 * M] = pltpu.roll(value, 1, 0).astype(BF16)
    halves(kf.at[pl.ds(0, 6)], dot(h1_t[...], m3[2 * WP : 2 * WP + NP, :]), 16, 16)
    halves(kf.at[pl.ds(12, 6)], dot(h1_t[...], m3[0:NP, :]), 16, 16)
    flight1 = core_phase(1)

    back[0:WP, :] += back_of(0, WP, 2)
    back[NP - WP : NP, :] += back_of(NP + WP, WP, 0)
    first_grad = jnp.where(h1p[...].astype(F32) > 0, back[...], 0.0).astype(BF16)
    first[...] = first_grad
    bh[0:8] = as_column(first_grad)
    in_next.wait()
    in_prev.wait()
    halves(d2, dot(in_t[...], first[...]), 16, 64)
    flight2 = core_phase(2)
    flight1 = first_phase(1, flight1)
    flight2 = first_phase(2, flight2)

    loads[7].wait()
    edge = dot_t1(first[...], win_v[0 : 2 * E, :])
    prod_e[...] = jnp.where(tm > 0, edge[:, 0:E], 0.0).astype(BF16)
    prod_l[...] = jnp.where(tm < n_tm - 1, edge[:, E:], 0.0).astype(BF16)
    early = send(prod_e, got_e, tm_prev)
    late = send(prod_l, got_l, tm_next)

    flight0 = second_phase(0, flight0)

    rest = og[:, 2 * E :].astype(F32) + dot_t1(first[...], win_v[2 * E :, :])
    for r in range(BAND):
        gi[r, :, 2 * E :] = rest[r * WP : r * WP + W].astype(BF16)
    flight1 = second_phase(1, flight1)
    flight0 = third_phase(0, flight0)
    early.wait()
    late.wait()
    for r in range(BAND):
        part = slice(r * WP, r * WP + WP)
        one = og[part, 0:E].astype(F32) + got_e[part, :].astype(F32)
        two = og[part, E : 2 * E].astype(F32) + got_l[part, :].astype(F32)
        gi[r, :, 0:E] = one[:W].astype(BF16)
        gi[r, :, E : 2 * E] = two[:W].astype(BF16)
    store = pltpu.make_async_copy(gi, gi_out, load_sem.at[8])
    store.start()

    flight1 = third_phase(1, flight1)
    flight2 = third_phase(2, flight2)
    last_phase(0, flight0, f0_out)
    last_phase(1, flight1, f1_out)
    last_phase(2, flight2, f2_out)
    store.wait()


def scratch():
    def v(*shape, dtype=BF16):
        return pltpu.VMEM(shape, dtype)

    shapes = [
        v(BAND, W, C), v(BAND, W, M), v(BAND, W, M), v(BAND, W, C), v(BAND, W, C),
        v(C, M), v(3, 3, M, M), v(M, C),
        v(NP, C), v(C, NP), v(NP, M + WP), v(NP, M), v(M, NP), v(NP + 2 * WP, 3 * M),
        v(C, NP), v(2, E, NP), v(NP, M), v(NP, M), v(2, WP, M), v(WP, M), v(WP, M),
        v(NP, E), v(NP, E), v(NP, E), v(NP, E), v(BAND, W, C),
        v(NP, M, dtype=F32), v(2, 16, 64, 128, dtype=F32), v(18, 16, 16, 128, dtype=F32), v(2, 16, 64, 128, dtype=F32),
        v(16, 64, WP, dtype=F32), v(16, 32, WP, dtype=F32),
    ]
    tile = (16, 128)
    for na, nb, depth in PIECES:
        shapes += [v(4, 4, na + nb, *tile), v(4, 4, na + nb, *tile)]
        if nb:
            shapes += [v(4, 4, na, *tile), v(3, 4, na, *tile), v(4, 4, nb, *tile), v(3, 4, nb, *tile)]
            shapes += [v(4, na, *tile), v(3, na, *tile), v(4, nb, *tile), v(3, nb, *tile)]
        else:
            shapes += [v(4, 4, na, *tile), v(15, na, *tile)]
        shapes += [v(8 * depth, 128, dtype=F32), v(7, depth, 128, dtype=F32)]
    shapes += [pltpu.SemaphoreType.DMA((9,)), pltpu.SemaphoreType.DMA((80,)), pltpu.SemaphoreType.DMA((80,))]
    return shapes


def finish(
    gi_in, f0_in, f1_in, f2_in, gi, d_in, d_mid, d_out, b_hidden, b_out,
    held, f0, f1, f2, d_in_v, d_mid_v, d_out_v, b_hidden_v, b_out_v, load_sem, store_sem,
):
    small = [(f0_in, f0), (f1_in, f1), (f2_in, f2)]
    large = [(gi_in.at[r], held.at[r]) for r in range(BAND)]
    loads = [pltpu.make_async_copy(src, dst, load_sem.at[i]) for i, (src, dst) in enumerate(large + small)]
    for load in loads:
        load.start()
    results = [(d_in_v, d_in), (d_mid_v, d_mid), (d_out_v, d_out), (b_hidden_v, b_hidden), (b_out_v, b_out)]
    results = [(held.at[r], gi.at[r]) for r in range(BAND)] + results
    stores = [pltpu.make_async_copy(src, dst, store_sem.at[i]) for i, (src, dst) in enumerate(results)]

    def lines(ref, start, count):
        return jnp.concatenate([ref[pl.ds(2 * start + h, count, stride=2), :] for h in range(2)], 1)

    for load in loads[BAND:]:
        load.wait()
    d_in_v[...] = lines(f2, 0, 4)
    d_mid_v[0] = lines(f1, 0, 3)
    d_mid_v[1] = lines(f0, 4, 3)
    d_mid_v[2] = lines(f1, 3, 3)
    d_out_v[...] = lines(f0, 0, 4)
    bias = f2[8, :] + f2[9, :]
    b_hidden_v[...] = bias[4:6]
    b_out_v[...] = bias[0:4]
    for store in stores[BAND:]:
        store.start()
    for load, store in zip(loads[:BAND], stores[:BAND]):
        load.wait()
        store.start()
    for store in stores:
        store.wait()


def on_device(inputs, hidden_one, hidden_two, outputs, cotangent, w_in, w_mid, w_out):
    anywhere = pl.BlockSpec(memory_space=pl.ANY)
    vmem = pl.BlockSpec(memory_space=pltpu.VMEM)
    gi, f0, f1, f2 = pl.pallas_call(
        kernel,
        out_shape=[
            jax.ShapeDtypeStruct((BAND, W, C), BF16),
            jax.ShapeDtypeStruct((PIECES[0][2], 128), F32),
            jax.ShapeDtypeStruct((PIECES[1][2], 128), F32),
            jax.ShapeDtypeStruct((PIECES[2][2], 128), F32),
        ],
        in_specs=[anywhere] * 8,
        out_specs=[anywhere, vmem, vmem, vmem],
        scratch_shapes=scratch(),
        compiler_params=pltpu.CompilerParams(
            collective_id=0, has_side_effects=True, vmem_limit_bytes=56 * 2**20
        ),
    )(inputs[0], hidden_one[0], hidden_two[0], outputs[0], cotangent[0], w_in, w_mid, w_out)
    gi, d_in, d_mid, d_out, b_hidden, b_out = pl.pallas_call(
        finish,
        out_shape=[
            jax.ShapeDtypeStruct((BAND, W, C), BF16),
            jax.ShapeDtypeStruct((4, M), F32),
            jax.ShapeDtypeStruct((3, 3, M), F32),
            jax.ShapeDtypeStruct((4, M), F32),
            jax.ShapeDtypeStruct((2,), F32),
            jax.ShapeDtypeStruct((4,), F32),
        ],
        in_specs=[anywhere] * 4,
        out_specs=[anywhere] * 6,
        scratch_shapes=[
            pltpu.VMEM((BAND, W, C), BF16),
            pltpu.VMEM((PIECES[0][2], 128), F32),
            pltpu.VMEM((PIECES[1][2], 128), F32),
            pltpu.VMEM((PIECES[2][2], 128), F32),
            pltpu.VMEM((4, M), F32),
            pltpu.VMEM((3, 3, M), F32),
            pltpu.VMEM((4, M), F32),
            pltpu.VMEM((2,), F32),
            pltpu.VMEM((4,), F32),
            pltpu.SemaphoreType.DMA((BAND + 3,)),
            pltpu.SemaphoreType.DMA((BAND + 5,)),
        ],
    )(gi, f0, f1, f2)
    return gi[None], d_in, d_mid, d_out.T, b_hidden, b_out


def solution(mesh):
    placed = (
        P("tm", "rows", None, None),
        P("tm", "rows", None, None),
        P("tm", "rows", None, None),
        P("tm", "rows", None, None),
        P("tm", "rows", None, None),
        P(),
        P(),
        P(),
    )
    return jax.shard_map(
        on_device,
        mesh=mesh,
        in_specs=placed,
        out_specs=(
            P("tm", "rows", None, None),
            P(("tm", "rows"), None),
            P(None, None, ("tm", "rows")),
            P(None, ("tm", "rows")),
            P(("tm", "rows")),
            P(("tm", "rows")),
        ),
        check_vma=False,
    )
```

time: 49.4 us -> 41.5 us (0.84)
  local copies, waits for them, and re-layouts: 4.61 us -> 0 us
  Pallas kernels: 43.9 us -> 40.2 us
    pallas_call x1, Pallas kernels: 42.6 us -> 37.8 us  [on_device(): pl.pallas_call(kernel, out_shape=[jax.ShapeDtypeStruct((BAND, W, C), BF16...]
    squeeze x2 -> x0, local copies, waits for them, and re-layouts: 2.4 us -> none  [on_device(): return (gi[None], d_in, d_mid, d_out.T, b_hidden[0, 4:6], b_out[0, 0:4])]
    unnamed x1 -> x0, local copies, waits for them, and re-layouts: 2.21 us -> none
    pallas_call x1, Pallas kernels: 1.33 us -> 2.32 us  [on_device(): pl.pallas_call(finish, out_shape=[jax.ShapeDtypeStruct((BAND, W, C), BF16...]
where the time goes in v2:
time: 41.5 us; the launch traced here: 40.8 us
  Pallas kernels  40.2 us (97%)
  between operations  0.64 us (2%)
    pallas_call x1, Pallas kernels, on_device(): pl.pallas_call(kernel, out_shape=[jax.ShapeDtypeStruct((BAND, W, C), BF16...  37.8 us
    pallas_call x1, Pallas kernels, on_device(): pl.pallas_call(finish, out_shape=[jax.ShapeDtypeStruct((BAND, W, C), BF16...  2.32 us

profile of v2, /device:TPU:2, one launch (start us, length us, event | category | flops | bytes accessed | tf_op | source)
XLA Modules:
  0.0 40.8 jit_solution(17757441219450880426)
XLA Ops:
  0.6 37.8 %shard_map.127 = (bf16[4,120,1024]{2,1,0:T(8,128)(2,1)}, f32[16,128]{1,0:T(8,128)}, f32[16,128]{1,0:T(8,128)}, f32[16,128]{1,0:T(8,128)}) custom-call(bf16[4,120,1024]{2,1,0:T(8,128)(2,1)} %bitcast.7, bf16[4,120,256]{2,1,0:T(8,128)(2,1)} %bitcast.10, bf16[4,120,256]{2,1,0:T(8,128)(2,1)} %bitcast.11, bf16[4,120,1024]{2,1,0:T(8,128)(2,1)} %bitcast.8, ...), custom_call_target="tpu_custom_call" | custom-call | tf_op jit(solution)/shard_map/pallas_call | solution.py:405
  38.5 2.3 %shard_map.128 = (bf16[4,120,1024]{2,1,0:T(8,128)(2,1)}, f32[4,256]{1,0:T(4,128)}, f32[3,3,256]{2,1,0:T(4,128)}, f32[4,256]{1,0:T(4,128)}, f32[2]{0:T(128)}, /*index=5*/f32[4]{0:T(128)}) custom-call(bf16[4,120,1024]{2,1,0:T(8,128)(2,1)} %get-tuple-element.16.gi_in, f32[16,128]{1,0:T(8,128)} %get-tuple-element.17.f0_in, f32[16,128]{1,0:T(8,128)} %get-tuple-element.18.f1_in, ...), custom_call_target="tpu_custom_call" | custom-call | tf_op jit(solution)/shard_map/pallas_call | solution.py:420

commit v3 on v2

--- a/solution.py
+++ b/solution.py
@@ -16,7 +16,8 @@
 C = 1024
 M = 256
 E = C // 8
-PIECES = ((4, 3, 16), (3, 3, 16), (5, 0, 16))
+PIECES = ((4, 3), (3, 3), (5, 0))
+DEPTH = 16
 
 
 def dot_t0(a, b):
@@ -33,13 +34,13 @@
 
 def kernel(
     inp, h1, h2, outp, cot, w_in, w_mid, w_out,
-    gi_out, f0_out, f1_out, f2_out,
+    gi_out, f0_out, f1_out, f2_out, f3_out,
     inp_v, h1_v, h2_v, outp_v, cot_v, win_v, wmid_v, wout_v,
     og, og_t, h2o, h1p, h1_t, m3, in_t, edge_t, first, mid_s, edge_mid, mup, mdn,
     prod_e, prod_l, got_e, got_l, gi, back, d0, kf, d2, bo, bh,
-    cs0, cr0, a1s0, a1r0, b1s0, b1r0, a2s0, a2r0, b2s0, b2r0, zs0, zr0,
-    cs1, cr1, a1s1, a1r1, b1s1, b1r1, a2s1, a2r1, b2s1, b2r1, zs1, zr1,
-    cs2, cr2, xys2, xyr2, zs2, zr2,
+    cs0, cr0, a1s0, a1r0, b1s0, b1r0, a2s0, a2r0, b2s0, b2r0, zf0, zs0, zr0,
+    cs1, cr1, a1s1, a1r1, b1s1, b1r1, a2s1, a2r1, b2s1, b2r1, zf1, zs1, zr1,
+    cs2, cr2, xys2, xyr2, zf2, zs2, zr2, zf3, zs3, zr3, sum3, xys3, xyr3,
     load_sem, send_sem, recv_sem,
 ):
     tm = lax.axis_index("tm")
@@ -144,9 +145,9 @@
         if piece == 0 and s >= 4 or piece == 1:
             tap = s - 1 if piece == 0 else s if s < 3 else s + 3
             parts = [kf[2 * tap + h, t, pl.ds(low, 8, stride=2), :] for h in range(2)]
-        elif s < 4:
-            held = d0 if piece == 0 else d2
-            parts = [held[h, t, pl.ds(4 * low + s, 8, stride=8), :] for h in range(2)]
+        elif piece == 0 or s != 2:
+            held, j = (d0, s) if piece == 0 else (d2, s - s // 3)
+            parts = [held[h, t, pl.ds(4 * low + j, 8, stride=8), :] for h in range(2)]
         else:
             lane = lax.broadcasted_iota(jnp.int32, (8, 128), 1)
             total = jnp.zeros((8, 128), F32)
@@ -163,13 +164,15 @@
         return jnp.concatenate([head, total - head], 0)
 
     bufs = (
-        (cs0, cr0, a1s0, a1r0, b1s0, b1r0, a2s0, a2r0, b2s0, b2r0, zs0, zr0),
-        (cs1, cr1, a1s1, a1r1, b1s1, b1r1, a2s1, a2r1, b2s1, b2r1, zs1, zr1),
-        (cs2, cr2, xys2, xyr2, None, None, None, None, None, None, zs2, zr2),
+        (cs0, cr0, a1s0, a1r0, b1s0, b1r0, a2s0, a2r0, b2s0, b2r0, zf0, zs0, zr0),
+        (cs1, cr1, a1s1, a1r1, b1s1, b1r1, a2s1, a2r1, b2s1, b2r1, zf1, zs1, zr1),
+        (cs2, cr2, xys2, xyr2, None, None, None, None, None, None, zf2, zs2, zr2),
     )
 
+    late3 = []
+
     def core_phase(p):
-        na, nb, _ = PIECES[p]
+        na, nb = PIECES[p]
         cs, cr = bufs[p][:2]
 
         def body(x, carry):
@@ -177,7 +180,7 @@
                 t = ((y // 2) * 4 + x) * 2 + (1 - core)
                 for s in range(na + nb):
                     value = slab(p, t, y % 2, s)
-                    if p == 2 and s == 4:
+                    if p == 2 and s == 2:
                         value = two_terms(value)
                     cs[x, y, s] = value.astype(BF16)
             return carry
@@ -186,7 +189,7 @@
         return [send(cs, cr, sibling)]
 
     def first_phase(p, copies):
-        na, nb, _ = PIECES[p]
+        na, nb = PIECES[p]
         cs, cr, a1s, a1r, b1s, b1r = bufs[p][:6]
         for copy in copies:
             copy.wait()
@@ -196,9 +199,13 @@
                 t = ((y // 2) * 4 + x) * 2 + core
                 for s in range(na + nb):
                     value = slab(p, t, y % 2, s) + cr[x, y, s].astype(F32)
-                    if p == 2 and s == 4:
+                    if p == 2 and s == 2:
                         value = two_terms(value)
-                    if s < na:
+                    if p == 2 and s > 2:
+                        for h in range(2):
+                            row = x * 16 + y * 4 + 2 * (s - 3) + h
+                            zf3[pl.ds(row, 8, stride=64), :] = value[8 * h : 8 * h + 8]
+                    elif s < na:
                         a1s[x, y, s] = value.astype(BF16)
                     else:
                         b1s[y, x, s - na] = value.astype(BF16)
@@ -207,6 +214,9 @@
         lax.fori_loop(0, 4, body, 0)
         out = []
         if p == 2:
+            zs3[...] = zf3[...].reshape(8, 64, 128).astype(BF16)
+            for k in (4, 3, 5, 2, 6, 1, 7):
+                late3.append(send(zs3.at[(mz + k) % 8], zr3.at[k - 1], z_peer[k - 1]))
             for (i, j), peer in sorted(xy_peer.items(), key=lambda item: -(item[0][0] % 3 + item[0][1] % 3)):
                 out.append(send(a1s.at[(mx + i) % 4, (my + j) % 4], a1r.at[4 * i + j - 1], peer))
             return out
@@ -222,7 +232,7 @@
         return total
 
     def second_phase(p, copies):
-        na, nb, _ = PIECES[p]
+        na, nb = PIECES[p]
         _, _, a1s, a1r, b1s, b1r, a2s, a2r, b2s, b2r = bufs[p][:10]
         for copy in copies:
             copy.wait()
@@ -236,34 +246,54 @@
         return out
 
     def third_phase(p, copies):
-        na, nb, depth = PIECES[p]
-        _, _, xys, xyr, _, _, a2s, a2r, b2s, b2r, zs, zr = bufs[p]
+        na, nb = PIECES[p]
+        _, _, xys, xyr, _, _, a2s, a2r, b2s, b2r, zf, zs, zr = bufs[p]
         for copy in copies:
             copy.wait()
-        for s in range(na + nb):
+        for s in range(3 if p == 2 else na + nb):
             if p == 2:
                 total = xys[mx, my, s].astype(F32)
                 for k in range(15):
                     total = total + xyr[k, s].astype(F32)
+                if s == 2:
+                    total = two_terms(total)
             else:
                 own, held, got, j = (my, a2s, a2r, s) if s < na else (mx, b2s, b2r, s - na)
                 total = gathered(own, held, got, j)
             for h in range(2):
-                zs[pl.ds(2 * s + h, 8, stride=depth), :] = total[8 * h : 8 * h + 8]
-        out = []
-        for k in (4, 3, 5, 2, 6, 1, 7):
-            start = pl.multiple_of(((mz + k) % 8) * depth, 8)
-            out.append(send(zs.at[pl.ds(start, depth)], zr.at[k - 1], z_peer[k - 1]))
-        return out
+                zf[pl.ds(2 * s + h, 8, stride=DEPTH), :] = total[8 * h : 8 * h + 8]
+        zs[...] = zf[...].reshape(8, DEPTH, 128).astype(BF16)
+        return [send(zs.at[(mz + k) % 8], zr.at[k - 1], z_peer[k - 1]) for k in (4, 3, 5, 2, 6, 1, 7)]
 
     def last_phase(p, copies, result):
-        depth = PIECES[p][2]
-        zs, zr = bufs[p][10:]
+        zf, _, zr = bufs[p][10:]
         for copy in copies:
             copy.wait()
-        total = zs[pl.ds(pl.multiple_of(mz * depth, 8), depth), :]
+        total = zf[pl.ds(pl.multiple_of(mz * DEPTH, 8), DEPTH), :]
         for k in range(7):
-            total = total + zr[k]
+            total = total + zr[k].astype(F32)
+        result[...] = total
+
+    def cross_phase(copies):
+        for copy in copies:
+            copy.wait()
+        total = zs3[mz].astype(F32)
+        for k in range(7):
+            total = total + zr3[k].astype(F32)
+        sum3[0:64, :] = total
+        for i in range(16):
+            xys3[i] = sum3[4 * i : 4 * i + 8, :]
+        out = []
+        for (i, j), peer in sorted(xy_peer.items(), key=lambda item: -(item[0][0] % 3 + item[0][1] % 3)):
+            out.append(send(xys3.at[((mx + i) % 4) * 4 + (my + j) % 4], xyr3.at[4 * i + j - 1], peer))
+        return out
+
+    def cross_end(copies, result):
+        for copy in copies:
+            copy.wait()
+        total = xys3[mx * 4 + my]
+        for k in range(15):
+            total = total + xyr3[k]
         result[...] = total
 
     flight0 = core_phase(0)
@@ -281,6 +311,8 @@
     back[WP:NP, :] += back_of(WP, NP - WP, 2)
 
     flight0 = first_phase(0, flight0)
+    halves(kf.at[pl.ds(0, 6)], dot(h1_t[:, 0 : NP - WP], m3[2 * WP : WP + NP, :]), 16, 16)
+    halves(kf.at[pl.ds(12, 6)], dot(h1_t[:, WP:NP], m3[WP:NP, :]), 16, 16)
 
     mid_down.wait()
     mid_up.wait()
@@ -289,21 +321,24 @@
         m3[start : start + WP, 0:M] = pltpu.roll(value, WP - 1, 0).astype(BF16)
         m3[start : start + WP, M : 2 * M] = held[...]
         m3[start : start + WP, 2 * M : 3 * M] = pltpu.roll(value, 1, 0).astype(BF16)
-    halves(kf.at[pl.ds(0, 6)], dot(h1_t[...], m3[2 * WP : 2 * WP + NP, :]), 16, 16)
-    halves(kf.at[pl.ds(12, 6)], dot(h1_t[...], m3[0:NP, :]), 16, 16)
+    for first_tap, grad in (
+        (0, dot(h1_t[:, NP - WP :], m3[NP + WP :, :])),
+        (12, dot(h1_t[:, 0:WP], m3[0:WP, :])),
+    ):
+        for h in range(6):
+            kf[first_tap + h] += grad[:, h * 128 : (h + 1) * 128].reshape(16, 16, 128)
     flight1 = core_phase(1)
 
     back[0:WP, :] += back_of(0, WP, 2)
     back[NP - WP : NP, :] += back_of(NP + WP, WP, 0)
     first_grad = jnp.where(h1p[...].astype(F32) > 0, back[...], 0.0).astype(BF16)
     first[...] = first_grad
+    flight1 = first_phase(1, flight1)
     bh[0:8] = as_column(first_grad)
     in_next.wait()
     in_prev.wait()
     halves(d2, dot(in_t[...], first[...]), 16, 64)
     flight2 = core_phase(2)
-    flight1 = first_phase(1, flight1)
-    flight2 = first_phase(2, flight2)
 
     loads[7].wait()
     edge = dot_t1(first[...], win_v[0 : 2 * E, :])
@@ -311,12 +346,12 @@
     prod_l[...] = jnp.where(tm < n_tm - 1, edge[:, E:], 0.0).astype(BF16)
     early = send(prod_e, got_e, tm_prev)
     late = send(prod_l, got_l, tm_next)
-
-    flight0 = second_phase(0, flight0)
+    flight2 = first_phase(2, flight2)
 
     rest = og[:, 2 * E :].astype(F32) + dot_t1(first[...], win_v[2 * E :, :])
     for r in range(BAND):
         gi[r, :, 2 * E :] = rest[r * WP : r * WP + W].astype(BF16)
+    flight0 = second_phase(0, flight0)
     flight1 = second_phase(1, flight1)
     flight0 = third_phase(0, flight0)
     early.wait()
@@ -330,11 +365,13 @@
     store = pltpu.make_async_copy(gi, gi_out, load_sem.at[8])
     store.start()
 
+    flight2 = third_phase(2, flight2)
+    flight3 = cross_phase(late3)
     flight1 = third_phase(1, flight1)
-    flight2 = third_phase(2, flight2)
     last_phase(0, flight0, f0_out)
+    last_phase(2, flight2, f2_out)
+    cross_end(flight3, f3_out)
     last_phase(1, flight1, f1_out)
-    last_phase(2, flight2, f2_out)
     store.wait()
 
 
@@ -352,23 +389,25 @@
         v(16, 64, WP, dtype=F32), v(16, 32, WP, dtype=F32),
     ]
     tile = (16, 128)
-    for na, nb, depth in PIECES:
+    for na, nb in PIECES:
         shapes += [v(4, 4, na + nb, *tile), v(4, 4, na + nb, *tile)]
         if nb:
             shapes += [v(4, 4, na, *tile), v(3, 4, na, *tile), v(4, 4, nb, *tile), v(3, 4, nb, *tile)]
             shapes += [v(4, na, *tile), v(3, na, *tile), v(4, nb, *tile), v(3, nb, *tile)]
         else:
-            shapes += [v(4, 4, na, *tile), v(15, na, *tile)]
-        shapes += [v(8 * depth, 128, dtype=F32), v(7, depth, 128, dtype=F32)]
-    shapes += [pltpu.SemaphoreType.DMA((9,)), pltpu.SemaphoreType.DMA((80,)), pltpu.SemaphoreType.DMA((80,))]
+            shapes += [v(4, 4, 3, *tile), v(15, 3, *tile)]
+        shapes += [v(8 * DEPTH, 128, dtype=F32), v(8, DEPTH, 128), v(7, DEPTH, 128)]
+    shapes += [v(8 * 64, 128, dtype=F32), v(8, 64, 128), v(7, 64, 128)]
+    shapes += [v(72, 128, dtype=F32), v(16, 8, 128, dtype=F32), v(15, 8, 128, dtype=F32)]
+    shapes += [pltpu.SemaphoreType.DMA((9,)), pltpu.SemaphoreType.DMA((100,)), pltpu.SemaphoreType.DMA((100,))]
     return shapes
 
 
 def finish(
-    gi_in, f0_in, f1_in, f2_in, gi, d_in, d_mid, d_out, b_hidden, b_out,
-    held, f0, f1, f2, d_in_v, d_mid_v, d_out_v, b_hidden_v, b_out_v, load_sem, store_sem,
+    gi_in, f0_in, f1_in, f2_in, f3_in, gi, d_in, d_mid, d_out, b_hidden, b_out,
+    held, f0, f1, f2, f3, d_in_v, d_mid_v, d_out_v, b_hidden_v, b_out_v, load_sem, store_sem,
 ):
-    small = [(f0_in, f0), (f1_in, f1), (f2_in, f2)]
+    small = [(f0_in, f0), (f1_in, f1), (f2_in, f2), (f3_in, f3)]
     large = [(gi_in.at[r], held.at[r]) for r in range(BAND)]
     loads = [pltpu.make_async_copy(src, dst, load_sem.at[i]) for i, (src, dst) in enumerate(large + small)]
     for load in loads:
@@ -382,12 +421,13 @@
 
     for load in loads[BAND:]:
         load.wait()
-    d_in_v[...] = lines(f2, 0, 4)
+    d_in_v[0:2, :] = lines(f2, 0, 2)
+    d_in_v[2:4, :] = lines(f3, 0, 2)
     d_mid_v[0] = lines(f1, 0, 3)
     d_mid_v[1] = lines(f0, 4, 3)
     d_mid_v[2] = lines(f1, 3, 3)
     d_out_v[...] = lines(f0, 0, 4)
-    bias = f2[8, :] + f2[9, :]
+    bias = f2[4, :] + f2[5, :]
     b_hidden_v[...] = bias[4:6]
     b_out_v[...] = bias[0:4]
     for store in stores[BAND:]:
@@ -402,16 +442,17 @@
 def on_device(inputs, hidden_one, hidden_two, outputs, cotangent, w_in, w_mid, w_out):
     anywhere = pl.BlockSpec(memory_space=pl.ANY)
     vmem = pl.BlockSpec(memory_space=pltpu.VMEM)
-    gi, f0, f1, f2 = pl.pallas_call(
+    gi, f0, f1, f2, f3 = pl.pallas_call(
         kernel,
         out_shape=[
             jax.ShapeDtypeStruct((BAND, W, C), BF16),
-            jax.ShapeDtypeStruct((PIECES[0][2], 128), F32),
-            jax.ShapeDtypeStruct((PIECES[1][2], 128), F32),
-            jax.ShapeDtypeStruct((PIECES[2][2], 128), F32),
+            jax.ShapeDtypeStruct((DEPTH, 128), F32),
+            jax.ShapeDtypeStruct((DEPTH, 128), F32),
+            jax.ShapeDtypeStruct((DEPTH, 128), F32),
+            jax.ShapeDtypeStruct((8, 128), F32),
         ],
         in_specs=[anywhere] * 8,
-        out_specs=[anywhere, vmem, vmem, vmem],
+        out_specs=[anywhere, vmem, vmem, vmem, vmem],
         scratch_shapes=scratch(),
         compiler_params=pltpu.CompilerParams(
             collective_id=0, has_side_effects=True, vmem_limit_bytes=56 * 2**20
@@ -427,22 +468,23 @@
             jax.ShapeDtypeStruct((2,), F32),
             jax.ShapeDtypeStruct((4,), F32),
         ],
-        in_specs=[anywhere] * 4,
+        in_specs=[anywhere] * 5,
         out_specs=[anywhere] * 6,
         scratch_shapes=[
             pltpu.VMEM((BAND, W, C), BF16),
-            pltpu.VMEM((PIECES[0][2], 128), F32),
-            pltpu.VMEM((PIECES[1][2], 128), F32),
-            pltpu.VMEM((PIECES[2][2], 128), F32),
+            pltpu.VMEM((DEPTH, 128), F32),
+            pltpu.VMEM((DEPTH, 128), F32),
+            pltpu.VMEM((DEPTH, 128), F32),
+            pltpu.VMEM((8, 128), F32),
             pltpu.VMEM((4, M), F32),
             pltpu.VMEM((3, 3, M), F32),
             pltpu.VMEM((4, M), F32),
             pltpu.VMEM((2,), F32),
             pltpu.VMEM((4,), F32),
-            pltpu.SemaphoreType.DMA((BAND + 3,)),
+            pltpu.SemaphoreType.DMA((BAND + 4,)),
             pltpu.SemaphoreType.DMA((BAND + 5,)),
         ],
-    )(gi, f0, f1, f2)
+    )(gi, f0, f1, f2, f3)
     return gi[None], d_in, d_mid, d_out.T, b_hidden, b_out
 
 

time: 41.5 us -> 40 us (0.964); the launches traced: 40.8 us -> 39.9 us
  Pallas kernels: 40.2 us -> 39.3 us
    pallas_call x1, Pallas kernels: 37.8 us -> 36.9 us  [on_device(): pl.pallas_call(kernel, out_shape=[jax.ShapeDtypeStruct((BAND, W, C), BF16...]
where the time goes in v3:
time: 40 us; the launch traced here: 39.9 us
  Pallas kernels  39.3 us (98%)
  between operations  0.64 us (2%)
    pallas_call x1, Pallas kernels, on_device(): pl.pallas_call(kernel, out_shape=[jax.ShapeDtypeStruct((BAND, W, C), BF16...  36.9 us
    pallas_call x1, Pallas kernels, on_device(): pl.pallas_call(finish, out_shape=[jax.ShapeDtypeStruct((BAND, W, C), BF16...  2.33 us

profile of v3, /device:TPU:2, one launch (start us, length us, event | category | flops | bytes accessed | tf_op | source)
XLA Modules:
  0.0 39.9 jit_solution(5008656064267018511)
XLA Ops:
  0.6 36.9 %shard_map.127 = (bf16[4,120,1024]{2,1,0:T(8,128)(2,1)}, f32[16,128]{1,0:T(8,128)}, f32[16,128]{1,0:T(8,128)}, f32[16,128]{1,0:T(8,128)}, f32[8,128]{1,0:T(8,128)}) custom-call(bf16[4,120,1024]{2,1,0:T(8,128)(2,1)} %bitcast.7, bf16[4,120,256]{2,1,0:T(8,128)(2,1)} %bitcast.10, bf16[4,120,256]{2,1,0:T(8,128)(2,1)} %bitcast.11, bf16[4,120,1024]{2,1,0:T(8,128)(2,1)} %bitcast.8, ...), custom_call_target="tpu_custom_call" | custom-call | tf_op jit(solution)/shard_map/pallas_call | solution.py:445
  37.6 2.3 %shard_map.128 = (bf16[4,120,1024]{2,1,0:T(8,128)(2,1)}, f32[4,256]{1,0:T(4,128)}, f32[3,3,256]{2,1,0:T(4,128)}, f32[4,256]{1,0:T(4,128)}, f32[2]{0:T(128)}, /*index=5*/f32[4]{0:T(128)}) custom-call(bf16[4,120,1024]{2,1,0:T(8,128)(2,1)} %get-tuple-element.17.gi_in, f32[16,128]{1,0:T(8,128)} %get-tuple-element.18.f0_in, f32[16,128]{1,0:T(8,128)} %get-tuple-element.19.f1_in, ...), custom_call_target="tpu_custom_call" | custom-call | tf_op jit(solution)/shard_map/pallas_call | solution.py:461

commit v4 on v3

--- a/solution.py
+++ b/solution.py
@@ -34,10 +34,10 @@
 
 def kernel(
     inp, h1, h2, outp, cot, w_in, w_mid, w_out,
-    gi_out, f0_out, f1_out, f2_out, f3_out,
+    gi, f0_out, f1_out, f2_out, f3_out,
     inp_v, h1_v, h2_v, outp_v, cot_v, win_v, wmid_v, wout_v,
     og, og_t, h2o, h1p, h1_t, m3, in_t, edge_t, first, mid_s, edge_mid, mup, mdn,
-    prod_e, prod_l, got_e, got_l, gi, back, d0, kf, d2, bo, bh,
+    prod_e, prod_l, got_e, got_l, back, d0, kf, d2, bo, bh,
     cs0, cr0, a1s0, a1r0, b1s0, b1r0, a2s0, a2r0, b2s0, b2r0, zf0, zs0, zr0,
     cs1, cr1, a1s1, a1r1, b1s1, b1r1, a2s1, a2r1, b2s1, b2r1, zf1, zs1, zr1,
     cs2, cr2, xys2, xyr2, zf2, zs2, zr2, zf3, zs3, zr3, sum3, xys3, xyr3,
@@ -362,8 +362,7 @@
         two = og[part, E : 2 * E].astype(F32) + got_l[part, :].astype(F32)
         gi[r, :, 0:E] = one[:W].astype(BF16)
         gi[r, :, E : 2 * E] = two[:W].astype(BF16)
-    store = pltpu.make_async_copy(gi, gi_out, load_sem.at[8])
-    store.start()
+
 
     flight2 = third_phase(2, flight2)
     flight3 = cross_phase(late3)
@@ -372,7 +371,6 @@
     last_phase(2, flight2, f2_out)
     cross_end(flight3, f3_out)
     last_phase(1, flight1, f1_out)
-    store.wait()
 
 
 def scratch():
@@ -384,7 +382,7 @@
         v(C, M), v(3, 3, M, M), v(M, C),
         v(NP, C), v(C, NP), v(NP, M + WP), v(NP, M), v(M, NP), v(NP + 2 * WP, 3 * M),
         v(C, NP), v(2, E, NP), v(NP, M), v(NP, M), v(2, WP, M), v(WP, M), v(WP, M),
-        v(NP, E), v(NP, E), v(NP, E), v(NP, E), v(BAND, W, C),
+        v(NP, E), v(NP, E), v(NP, E), v(NP, E),
         v(NP, M, dtype=F32), v(2, 16, 64, 128, dtype=F32), v(18, 16, 16, 128, dtype=F32), v(2, 16, 64, 128, dtype=F32),
         v(16, 64, WP, dtype=F32), v(16, 32, WP, dtype=F32),
     ]
@@ -404,14 +402,9 @@
 
 
 def finish(
-    gi_in, f0_in, f1_in, f2_in, f3_in, gi, d_in, d_mid, d_out, b_hidden, b_out,
-    held, f0, f1, f2, f3, d_in_v, d_mid_v, d_out_v, b_hidden_v, b_out_v, load_sem, store_sem,
+    held, f0, f1, f2, f3, gi, d_in, d_mid, d_out, b_hidden, b_out,
+    d_in_v, d_mid_v, d_out_v, b_hidden_v, b_out_v, store_sem,
 ):
-    small = [(f0_in, f0), (f1_in, f1), (f2_in, f2), (f3_in, f3)]
-    large = [(gi_in.at[r], held.at[r]) for r in range(BAND)]
-    loads = [pltpu.make_async_copy(src, dst, load_sem.at[i]) for i, (src, dst) in enumerate(large + small)]
-    for load in loads:
-        load.start()
     results = [(d_in_v, d_in), (d_mid_v, d_mid), (d_out_v, d_out), (b_hidden_v, b_hidden), (b_out_v, b_out)]
     results = [(held.at[r], gi.at[r]) for r in range(BAND)] + results
     stores = [pltpu.make_async_copy(src, dst, store_sem.at[i]) for i, (src, dst) in enumerate(results)]
@@ -419,8 +412,8 @@
     def lines(ref, start, count):
         return jnp.concatenate([ref[pl.ds(2 * start + h, count, stride=2), :] for h in range(2)], 1)
 
-    for load in loads[BAND:]:
-        load.wait()
+    for store in stores[:BAND]:
+        store.start()
     d_in_v[0:2, :] = lines(f2, 0, 2)
     d_in_v[2:4, :] = lines(f3, 0, 2)
     d_mid_v[0] = lines(f1, 0, 3)
@@ -432,9 +425,6 @@
     b_out_v[...] = bias[0:4]
     for store in stores[BAND:]:
         store.start()
-    for load, store in zip(loads[:BAND], stores[:BAND]):
-        load.wait()
-        store.start()
     for store in stores:
         store.wait()
 
@@ -445,14 +435,14 @@
     gi, f0, f1, f2, f3 = pl.pallas_call(
         kernel,
         out_shape=[
-            jax.ShapeDtypeStruct((BAND, W, C), BF16),
-            jax.ShapeDtypeStruct((DEPTH, 128), F32),
-            jax.ShapeDtypeStruct((DEPTH, 128), F32),
-            jax.ShapeDtypeStruct((DEPTH, 128), F32),
-            jax.ShapeDtypeStruct((8, 128), F32),
+            pltpu.VMEM((BAND, W, C), BF16),
+            pltpu.VMEM((DEPTH, 128), F32),
+            pltpu.VMEM((DEPTH, 128), F32),
+            pltpu.VMEM((DEPTH, 128), F32),
+            pltpu.VMEM((8, 128), F32),
         ],
         in_specs=[anywhere] * 8,
-        out_specs=[anywhere, vmem, vmem, vmem, vmem],
+        out_specs=[vmem] * 5,
         scratch_shapes=scratch(),
         compiler_params=pltpu.CompilerParams(
             collective_id=0, has_side_effects=True, vmem_limit_bytes=56 * 2**20
@@ -468,22 +458,17 @@
             jax.ShapeDtypeStruct((2,), F32),
             jax.ShapeDtypeStruct((4,), F32),
         ],
-        in_specs=[anywhere] * 5,
+        in_specs=[vmem] * 5,
         out_specs=[anywhere] * 6,
         scratch_shapes=[
-            pltpu.VMEM((BAND, W, C), BF16),
-            pltpu.VMEM((DEPTH, 128), F32),
-            pltpu.VMEM((DEPTH, 128), F32),
-            pltpu.VMEM((DEPTH, 128), F32),
-            pltpu.VMEM((8, 128), F32),
             pltpu.VMEM((4, M), F32),
             pltpu.VMEM((3, 3, M), F32),
             pltpu.VMEM((4, M), F32),
             pltpu.VMEM((2,), F32),
             pltpu.VMEM((4,), F32),
-            pltpu.SemaphoreType.DMA((BAND + 4,)),
             pltpu.SemaphoreType.DMA((BAND + 5,)),
         ],
+        compiler_params=pltpu.CompilerParams(vmem_limit_bytes=8 * 2**20),
     )(gi, f0, f1, f2, f3)
     return gi[None], d_in, d_mid, d_out.T, b_hidden, b_out
 

time: 40 us -> 38.1 us (0.953)
  Pallas kernels: 39.3 us -> 37.3 us
    pallas_call x1, Pallas kernels: 2.33 us -> 1.03 us  [on_device(): pl.pallas_call(finish, out_shape=[jax.ShapeDtypeStruct((BAND, W, C), BF16...]
    pallas_call x1, Pallas kernels: 36.9 us -> 36.3 us  [on_device(): pl.pallas_call(kernel, out_shape=[pltpu.VMEM((BAND, W, C), BF16), pltpu.V...]
where the time goes in v4:
time: 38.1 us; the launch traced here: 38 us
  Pallas kernels  37.3 us (98%)
  between operations  0.64 us (2%)
    pallas_call x1, Pallas kernels, on_device(): pl.pallas_call(kernel, out_shape=[pltpu.VMEM((BAND, W, C), BF16), pltpu.V...  36.3 us
    pallas_call x1, Pallas kernels, on_device(): pl.pallas_call(finish, out_shape=[jax.ShapeDtypeStruct((BAND, W, C), BF16...  1.03 us

profile of v4, /device:TPU:2, one launch (start us, length us, event | category | flops | bytes accessed | tf_op | source)
XLA Modules:
  0.0 38.0 jit_solution(665225939076462997)
XLA Ops:
  0.6 36.3 %shard_map.127 = (bf16[4,120,1024]{2,1,0:T(8,128)(2,1)S(1)}, f32[16,128]{1,0:T(8,128)S(1)}, f32[16,128]{1,0:T(8,128)S(1)}, f32[16,128]{1,0:T(8,128)S(1)}, f32[8,128]{1,0:T(8,128)S(1)}) custom-call(bf16[4,120,1024]{2,1,0:T(8,128)(2,1)} %bitcast.7, bf16[4,120,256]{2,1,0:T(8,128)(2,1)} %bitcast.10, bf16[4,120,256]{2,1,0:T(8,128)(2,1)} %bitcast.11, ...), custom_call_target="tpu_custom_call" | custom-call | tf_op jit(solution)/shard_map/pallas_call | solution.py:435
  36.9 1.0 %shard_map.128 = (bf16[4,120,1024]{2,1,0:T(8,128)(2,1)}, f32[4,256]{1,0:T(4,128)}, f32[3,3,256]{2,1,0:T(4,128)}, f32[4,256]{1,0:T(4,128)}, f32[2]{0:T(128)}, /*index=5*/f32[4]{0:T(128)}) custom-call(bf16[4,120,1024]{2,1,0:T(8,128)(2,1)S(1)} %get-tuple-element.17.held, f32[16,128]{1,0:T(8,128)S(1)} %get-tuple-element.18.f0, ...), custom_call_target="tpu_custom_call" | custom-call | tf_op jit(solution)/shard_map/pallas_call | solution.py:451

commit v5 on v4

--- a/solution.py
+++ b/solution.py
@@ -117,6 +117,19 @@
     m3[WP : WP + NP, M : 2 * M] = mid
     m3[WP : WP + NP, 2 * M : 3 * M] = pltpu.roll(mid32, 1, 0).astype(BF16)
 
+    pl.semaphore_wait(barrier, len(partners))
+    mid_down = send(edge_mid.at[0], mup, row_next)
+    mid_up = send(edge_mid.at[1], mdn, row_prev)
+
+    loads[5].wait()
+    for r in range(BAND):
+        part = slice(r * WP, (r + 1) * WP)
+        value = pad_rows(inp_v[r].astype(F32)).T
+        edge_t[0, :, part] = jnp.where(tm < n_tm - 1, value[0:E].astype(F32), 0.0).astype(BF16)
+        edge_t[1, :, part] = jnp.where(tm > 0, value[E : 2 * E].astype(F32), 0.0).astype(BF16)
+        in_t[2 * E :, part] = value[2 * E :]
+    in_next = send(edge_t.at[0], in_t.at[pl.ds(0, E)], tm_next)
+    in_prev = send(edge_t.at[1], in_t.at[pl.ds(E, E)], tm_prev)
     og_t[...] = og[...].T
     grad = dot(og_t[...], h2o[...])
     halves(d0, grad[:, 0:M], 16, 64)
@@ -127,20 +140,6 @@
         h1p[r * WP : (r + 1) * WP, :] = pad_rows(h1_v[r].astype(F32))
     h1_t[...] = h1p[...].T
     halves(kf.at[pl.ds(6, 6)], dot(h1_t[...], m3[WP : WP + NP, :]), 16, 16)
-    loads[5].wait()
-    for r in range(BAND):
-        part = slice(r * WP, (r + 1) * WP)
-        value = pad_rows(inp_v[r].astype(F32)).T
-        edge_t[0, :, part] = jnp.where(tm < n_tm - 1, value[0:E].astype(F32), 0.0).astype(BF16)
-        edge_t[1, :, part] = jnp.where(tm > 0, value[E : 2 * E].astype(F32), 0.0).astype(BF16)
-        in_t[2 * E :, part] = value[2 * E :]
-
-    pl.semaphore_wait(barrier, len(partners))
-    mid_down = send(edge_mid.at[0], mup, row_next)
-    mid_up = send(edge_mid.at[1], mdn, row_prev)
-    in_next = send(edge_t.at[0], in_t.at[pl.ds(0, E)], tm_next)
-    in_prev = send(edge_t.at[1], in_t.at[pl.ds(E, E)], tm_prev)
-
     def slab(piece, t, low, s):
         if piece == 0 and s >= 4 or piece == 1:
             tap = s - 1 if piece == 0 else s if s < 3 else s + 3

time: 38.1 us -> 36.6 us (0.961)
  Pallas kernels: 37.3 us -> 35.5 us
    pallas_call x1, Pallas kernels: 36.3 us -> 34.5 us  [on_device(): pl.pallas_call(kernel, out_shape=[pltpu.VMEM((BAND, W, C), BF16), pltpu.V...]
where the time goes in v5:
time: 36.6 us; the launch traced here: 36.2 us
  Pallas kernels  35.5 us (97%)
  between operations  0.64 us (2%)
    pallas_call x1, Pallas kernels, on_device(): pl.pallas_call(kernel, out_shape=[pltpu.VMEM((BAND, W, C), BF16), pltpu.V...  34.5 us
    pallas_call x1, Pallas kernels, on_device(): pl.pallas_call(finish, out_shape=[jax.ShapeDtypeStruct((BAND, W, C), BF16...  1.03 us

profile of v5, /device:TPU:2, one launch (start us, length us, event | category | flops | bytes accessed | tf_op | source)
XLA Modules:
  0.0 36.2 jit_solution(6864480849857301731)
XLA Ops:
  0.6 34.5 %shard_map.127 = (bf16[4,120,1024]{2,1,0:T(8,128)(2,1)S(1)}, f32[16,128]{1,0:T(8,128)S(1)}, f32[16,128]{1,0:T(8,128)S(1)}, f32[16,128]{1,0:T(8,128)S(1)}, f32[8,128]{1,0:T(8,128)S(1)}) custom-call(bf16[4,120,1024]{2,1,0:T(8,128)(2,1)} %bitcast.7, bf16[4,120,256]{2,1,0:T(8,128)(2,1)} %bitcast.10, bf16[4,120,256]{2,1,0:T(8,128)(2,1)} %bitcast.11, ...), custom_call_target="tpu_custom_call" | custom-call | tf_op jit(solution)/shard_map/pallas_call | solution.py:434
  35.1 1.0 %shard_map.128 = (bf16[4,120,1024]{2,1,0:T(8,128)(2,1)}, f32[4,256]{1,0:T(4,128)}, f32[3,3,256]{2,1,0:T(4,128)}, f32[4,256]{1,0:T(4,128)}, f32[2]{0:T(128)}, /*index=5*/f32[4]{0:T(128)}) custom-call(bf16[4,120,1024]{2,1,0:T(8,128)(2,1)S(1)} %get-tuple-element.17.held, f32[16,128]{1,0:T(8,128)S(1)} %get-tuple-element.18.f0, ...), custom_call_target="tpu_custom_call" | custom-call | tf_op jit(solution)/shard_map/pallas_call | solution.py:450

commit v6 on v5

--- a/solution.py
+++ b/solution.py
@@ -332,12 +332,12 @@
     back[NP - WP : NP, :] += back_of(NP + WP, WP, 0)
     first_grad = jnp.where(h1p[...].astype(F32) > 0, back[...], 0.0).astype(BF16)
     first[...] = first_grad
-    flight1 = first_phase(1, flight1)
     bh[0:8] = as_column(first_grad)
     in_next.wait()
     in_prev.wait()
     halves(d2, dot(in_t[...], first[...]), 16, 64)
     flight2 = core_phase(2)
+    flight1 = first_phase(1, flight1)
 
     loads[7].wait()
     edge = dot_t1(first[...], win_v[0 : 2 * E, :])

time: 36.6 us -> 36.1 us (0.986)
  no operation moved by 1% of the time
where the time goes in v6:
time: 36.1 us; the launch traced here: 36 us
  Pallas kernels  35.4 us (98%)
  between operations  0.64 us (2%)
    pallas_call x1, Pallas kernels, on_device(): pl.pallas_call(kernel, out_shape=[pltpu.VMEM((BAND, W, C), BF16), pltpu.V...  34.4 us
    pallas_call x1, Pallas kernels, on_device(): pl.pallas_call(finish, out_shape=[jax.ShapeDtypeStruct((BAND, W, C), BF16...  1.03 us

profile of v6, /device:TPU:2, one launch (start us, length us, event | category | flops | bytes accessed | tf_op | source)
XLA Modules:
  0.0 36.0 jit_solution(12084718425300329298)
XLA Ops:
  0.6 34.4 %shard_map.127 = (bf16[4,120,1024]{2,1,0:T(8,128)(2,1)S(1)}, f32[16,128]{1,0:T(8,128)S(1)}, f32[16,128]{1,0:T(8,128)S(1)}, f32[16,128]{1,0:T(8,128)S(1)}, f32[8,128]{1,0:T(8,128)S(1)}) custom-call(bf16[4,120,1024]{2,1,0:T(8,128)(2,1)} %bitcast.7, bf16[4,120,256]{2,1,0:T(8,128)(2,1)} %bitcast.10, bf16[4,120,256]{2,1,0:T(8,128)(2,1)} %bitcast.11, ...), custom_call_target="tpu_custom_call" | custom-call | tf_op jit(solution)/shard_map/pallas_call | solution.py:434
  35.0 1.0 %shard_map.128 = (bf16[4,120,1024]{2,1,0:T(8,128)(2,1)}, f32[4,256]{1,0:T(4,128)}, f32[3,3,256]{2,1,0:T(4,128)}, f32[4,256]{1,0:T(4,128)}, f32[2]{0:T(128)}, /*index=5*/f32[4]{0:T(128)}) custom-call(bf16[4,120,1024]{2,1,0:T(8,128)(2,1)S(1)} %get-tuple-element.17.held, f32[16,128]{1,0:T(8,128)S(1)} %get-tuple-element.18.f0, ...), custom_call_target="tpu_custom_call" | custom-call | tf_op jit(solution)/shard_map/pallas_call | solution.py:450
